TPU v7x, 256 devices: a whole 4x4x8 slice. The times are simulated.
256 devices in a mesh: grp: 2 (over z_hi), az: 64 (over x, z_lo, y), ax: 2 (over core).
Axes of the slice: x: 4, y: 4, z: 8 (z_hi: 2, z_lo: 4; z = z_hi * 4 + z_lo), core: 2. Of those that a mesh axis runs over, the one named last changes fastest.
Arguments:
- cavity_block: float32 [8, 96, 256, 256], P(None, 'grp', 'az', 'ax'), may hold values from -95 to 95
- shell_block: float32 [8, 6, 256, 256], P(None, None, 'az', 'ax'), may hold values from -95 to 95
- column_matrix: float32 [2, 48, 48], P('grp'), may hold values from -2 to 6, as said below
- shell_matrix: float32 [6, 6], replicated, may hold values from -2 to 6, as said below
- shifted_diagonal: float32 [96, 256, 256], P('grp', 'az', 'ax'), may hold values from 1.6 to 3
- shell_diagonal: float32 [6, 256, 256], P(None, 'az', 'ax'), may hold values from 1.6 to 3
- wet_area: float32 [256, 256], P('az', 'ax'), may hold values from 0.3 to 1.5
Outputs:
- cavity_solution: float32 [8, 96, 256, 256], P(None, 'grp', 'az', 'ax')
- cavity_residual: float32 [8, 96, 256, 256], P(None, 'grp', 'az', 'ax')
- shell_solution: float32 [8, 6, 256, 256], P(None, None, 'az', 'ax')
- shell_residual: float32 [8, 6, 256, 256], P(None, None, 'az', 'ax')
Inputs may be any that keep to these rules, and one draw needn't show every extreme that they name: `column_matrix`: each symmetric and positive definite. `shell_matrix`: symmetric and positive definite.
All inputs are finite; a program needn't handle non-finite values.
Results may differ from a plain program's by a relative error of at most 0.0015.
Values sent between devices are 32-bit elements; how exact they have to be, the bound alone decides.
A program may use at most 128 MiB of HBM per device.

v0:
```python
import jax
import jax.numpy as jnp
from jax import lax
from jax.experimental import pallas as pl
from jax.experimental.pallas import tpu as pltpu
from jax.sharding import PartitionSpec as P

NV = 8
RC = 48
RS = 6
ROWS = 56
AZL = 4
BLK = AZL * ROWS
STEPS = 3
THETA = 9.0
MESH = pl.DeviceIdType.MESH
F32 = jnp.float32
BF16 = jnp.bfloat16


def rounded(value):
    return value.astype(BF16).astype(F32)


def kernel(
    cav, shl, colm, shm, dia, sdia, wet,
    sol_c, res_c, sol_s, res_s,
    X, HL, HR, SB, IS, IR, DG, W, STG, ACC, RX1, RX2,
    raw_c, raw_s, raw_d, raw_sd, raw_w, raw_cm, raw_sm,
    o_sc, o_rc, o_ss, o_rs,
    in_sem, out_sem, send_sem, recv_sem, s1, r1, s2, r2,
):
    grp = lax.axis_index("grp")
    az = lax.axis_index("az")
    ax = lax.axis_index("ax")
    naz = 64
    right = lax.rem(az + 1, naz)
    left = lax.rem(az + naz - 1, naz)
    px = az // 16
    pz = lax.rem(az // 4, 4)
    py = lax.rem(az, 4)

    loads = [
        pltpu.make_async_copy(src, dst, in_sem.at[i])
        for i, (src, dst) in enumerate(
            [(cav, raw_c), (shl, raw_s), (dia, raw_d), (sdia, raw_sd), (wet, raw_w), (colm, raw_cm), (shm, raw_sm)]
        )
    ]
    for load in loads:
        load.start()

    barrier = pltpu.get_barrier_semaphore()

    def hello(where):
        pl.semaphore_signal(barrier, inc=1, device_id=where, device_id_type=MESH)

    me1 = px * 4 + py
    me2 = grp * 8 + pz * 2 + ax

    def peer1(d):
        s = lax.rem(me1 + d, 16)
        return s, {"grp": grp, "az": (s // 4) * 16 + pz * 4 + lax.rem(s, 4), "ax": ax}

    def peer2(d):
        s = lax.rem(me2 + d, 16)
        return s, {"grp": s // 8, "az": px * 16 + lax.rem(s // 2, 4) * 4 + py, "ax": lax.rem(s, 2)}

    to_right = {"grp": grp, "az": right, "ax": ax}
    to_left = {"grp": grp, "az": left, "ax": ax}
    to_core = {"grp": grp, "az": az, "ax": 1 - ax}
    to_half = {"grp": 1 - grp, "az": az, "ax": ax}
    for where in (to_right, to_left, to_core, to_half):
        hello(where)

    def hello_peers(d, c):
        hello(peer1(d)[1])
        hello(peer2(d)[1])
        return c

    lax.fori_loop(1, 16, hello_peers, 0)

    outer = (grp == 1).astype(F32)
    is_outer = grp == 1
    lane = lax.broadcasted_iota(jnp.int32, (8, 128), 1)
    row = lax.broadcasted_iota(jnp.int32, (8, 128), 0)

    for load in loads:
        load.wait()

    def place(v, c):
        for a in range(AZL):
            at = v * BLK + a * ROWS
            X[0, pl.ds(pl.multiple_of(at, 8), RC), :] = raw_c[pl.ds(v * (RC * AZL) + a, RC, stride=AZL), :]
            tail = jnp.concatenate(
                [raw_s[pl.ds(v * (RS * AZL) + a, RS, stride=AZL), :], jnp.zeros((2, 128), F32)], axis=0
            )
            X[0, pl.ds(pl.multiple_of(at + RC, 8), 8), :] = tail
        return c

    lax.fori_loop(0, NV, place, 0)

    def rows_to_send(k, v):
        for a in range(AZL):
            at = v * BLK + a * ROWS
            first = X[k, pl.ds(pl.multiple_of(at, 8), 8), :][0:1]
            last = X[k, pl.ds(pl.multiple_of(at + 40, 8), 8), :][7:8]
            IS[k, v, a : a + 1, :] = jnp.where(is_outer, first, last)
            IS[k, v, 4 + a : 5 + a, :] = last

    def exchange(k, v):
        base = pl.multiple_of(v * BLK, 8)
        top = pl.multiple_of(v * BLK + 3 * ROWS, 8)
        return (
            pltpu.make_async_remote_copy(
                X.at[k, pl.ds(top, ROWS), :], HL.at[k, v], send_sem.at[k, 0], recv_sem.at[k, v, 0],
                device_id=to_right, device_id_type=MESH,
            ),
            pltpu.make_async_remote_copy(
                X.at[k, pl.ds(base, ROWS), :], HR.at[k, v], send_sem.at[k, 1], recv_sem.at[k, v, 1],
                device_id=to_left, device_id_type=MESH,
            ),
            pltpu.make_async_remote_copy(
                X.at[k, pl.ds(base, BLK), :], SB.at[k, v], send_sem.at[k, 2], recv_sem.at[k, v, 2],
                device_id=to_core, device_id_type=MESH,
            ),
            pltpu.make_async_remote_copy(
                IS.at[k, v], IR.at[k, v], send_sem.at[k, 3], recv_sem.at[k, v, 3],
                device_id=to_half, device_id_type=MESH,
            ),
        )

    def sent(k):
        for i, (buf, where) in enumerate(((HL, to_right), (HR, to_left), (SB, to_core), (IS, to_half))):
            pltpu.make_async_remote_copy(
                buf.at[k], buf.at[k], send_sem.at[k, i], recv_sem.at[k, 0, i], device_id=where, device_id_type=MESH
            ).wait_send()

    pl.semaphore_wait(barrier, 34)

    def first_send(v, c):
        rows_to_send(0, v)
        for copy in exchange(0, v):
            copy.start()
        return c

    lax.fori_loop(0, NV, first_send, 0)

    for a in range(AZL):
        DG[a, 0:RC, :] = raw_d[pl.ds(a, RC, stride=AZL), :] + (4.0 - THETA)
        DG[a, RC:ROWS, :] = jnp.concatenate(
            [raw_sd[pl.ds(a, RS, stride=AZL), :] + (4.0 - THETA), jnp.zeros((2, 128), F32)], axis=0
        )
    STG[...] = jnp.zeros((64, 128), F32)
    STG[56:62, 0:RS] = raw_sm[...]
    shell_rows = pltpu.roll(STG[56:64, :], RC, axis=1)
    STG[56:64, :] = jnp.zeros((8, 128), F32)
    STG[0:RC, 0:RC] = raw_cm[...]
    STG[RC:ROWS, :] = shell_rows
    row64 = lax.broadcasted_iota(jnp.int32, (64, 128), 0)
    lane64 = lax.broadcasted_iota(jnp.int32, (64, 128), 1)
    iface = jnp.where(is_outer, 0, RC - 1)
    matrix = STG[...]
    matrix = jnp.where((lane64 == 56) & (row64 == iface), -1.0, matrix)
    matrix = jnp.where((lane64 == 57) & (row64 == RC), -1.0, matrix)
    matrix = jnp.where((lane64 == 58) & (row64 == RC - 1), -outer, matrix)
    high = rounded(matrix)
    W[...] = jnp.concatenate([high + pltpu.roll(high, 64, axis=1), matrix - high], axis=1).astype(BF16)

    lane56 = lax.broadcasted_iota(jnp.int32, (ROWS, 128), 1)
    first_lane = lane56 == 0
    last_lane = lane56 == 127
    from_left = (ax == 1).astype(F32)
    from_right = (ax == 0).astype(F32)
    share = 1.0 - outer

    def apply(k):
        def body(v, moments):
            base = v * BLK
            for copy in exchange(k, v):
                copy.wait_recv()
            own = [X[k, pl.ds(pl.multiple_of(base + a * ROWS, 8), ROWS), :] for a in range(AZL)]
            got = IR[k, v]
            spread = []
            for a in range(AZL):
                wet_row = raw_w[a : a + 1, :]
                wall = jnp.where(is_outer, own[a][RC - 1 : RC], got[4 + a : 5 + a])
                skin = own[a][RC : RC + 1]
                extra = jnp.where(row == 0, got[a : a + 1], 0.0)
                extra = jnp.where(row == 1, wet_row * wall, extra)
                extra = jnp.where(row == 2, wet_row * skin, extra)
                spread.append(jnp.concatenate([own[a], extra], axis=0))
            wide = jnp.concatenate(spread, axis=1)
            high = rounded(wide)
            stacked = jnp.concatenate([high, wide - high, high], axis=0).astype(BF16)
            mixed = jnp.dot(W[:, 0:192], stacked, preferred_element_type=F32)
            for a in range(AZL):
                side = SB[k, v, a * ROWS : (a + 1) * ROWS, :]
                before = HL[k, v] if a == 0 else own[a - 1]
                after = HR[k, v] if a == AZL - 1 else own[a + 1]
                lower = pltpu.roll(jnp.where(last_lane, side * from_left, own[a]), 1, axis=1)
                upper = pltpu.roll(jnp.where(first_lane, side * from_right, own[a]), 127, axis=1)
                new = mixed[0:ROWS, a * 128 : (a + 1) * 128] + DG[a] * own[a]
                new = new - ((before + after) + (lower + upper))
                X[k + 1, pl.ds(pl.multiple_of(base + a * ROWS, 8), ROWS), :] = new
            if k + 1 < STEPS:
                rows_to_send(k + 1, v)
                for copy in exchange(k + 1, v):
                    copy.start()
            even = [jnp.zeros((8, 128), F32) for _ in range(NV)]
            odd = [jnp.zeros((8, 128), F32) for _ in range(NV)]
            for p in range(BLK // 8):
                here = pl.ds(pl.multiple_of(base + p * 8, 8), 8)
                old, new = X[k, here, :], X[k + 1, here, :]
                if p % 7 == 6:
                    old, new = old * share, new * share
                for w in range(NV):
                    other = X[k, w * BLK + p * 8 : w * BLK + p * 8 + 8, :]
                    even[w] += other * old
                    odd[w] += other * new
            for w in range(NV):
                ACC[w * 8 : w * 8 + 8, :] = even[w]
                ACC[64 + w * 8 : 72 + w * 8, :] = odd[w]
            for half in range(2):
                total = ACC[pl.ds(64 * half, 8, stride=8), :]
                for s in range(1, 8):
                    total += ACC[pl.ds(64 * half + s, 8, stride=8), :]
                total = jnp.sum(total, axis=1, keepdims=True)
                moments = jnp.where(lane == 8 * (2 * k + half) + v, total, moments)
            return moments

        return body

    moments = jnp.zeros((8, 128), F32)
    for k in range(STEPS):
        moments = lax.fori_loop(0, NV, apply(k), moments)

    def total_of(value, me, peer, buf, ssem, rsem):
        buf[me] = value

        def copy_of(d):
            s, where = peer(d)
            return s, pltpu.make_async_remote_copy(
                buf.at[me], buf.at[me], ssem.at[d], rsem.at[me], device_id=where, device_id_type=MESH
            )

        def start(d, c):
            copy_of(d)[1].start()
            return c

        def wait(d, c):
            s, where = peer(d)
            pltpu.make_async_remote_copy(
                buf.at[s], buf.at[s], ssem.at[d], rsem.at[s], device_id=where, device_id_type=MESH
            ).wait_recv()
            return c

        def drain(d, c):
            copy_of(d)[1].wait_send()
            return c

        lax.fori_loop(1, 16, start, 0)
        lax.fori_loop(1, 16, wait, 0)
        result = buf[0]
        for s in range(1, 16):
            result += buf[s]
        lax.fori_loop(1, 16, drain, 0)
        return result

    gram = total_of(moments, me1, peer1, RX1, s1, r1)
    gram = total_of(gram, me2, peer2, RX2, s2, r2)

    shifted = pltpu.roll(gram, 120, axis=1) + THETA * gram
    table = []
    for i in range(STEPS):
        left_part = shifted if i == 0 else pltpu.roll(shifted, 128 - 8 * i, axis=1)
        right_part = pltpu.roll(gram, 24 - 8 * i, axis=1)
        table.append(jnp.where(lane < 24, left_part, jnp.where(lane < 32, right_part, 0.0)))
    for p in range(8 * STEPS):
        at, r = p // 8, p % 8
        pivot_row = table[at][r : r + 1, :]
        scaled = pivot_row * (1.0 / pivot_row[:, p : p + 1])
        for i in range(STEPS):
            column = table[i][:, p : p + 1]
            reduced = table[i] - column * scaled
            table[i] = jnp.where(row == r, scaled, reduced) if i == at else reduced

    y = [jnp.where(lane < 8, pltpu.roll(t, 104, axis=1), 0.0) for t in table]
    eye = jnp.where(lane == row, 1.0, 0.0)
    into = [
        eye - THETA * y[0],
        -(y[0] + THETA * y[1]),
        -(y[1] + THETA * y[2]),
        -y[2],
    ]
    zero8 = jnp.zeros((8, 128), F32)
    parts = [(y[k] if k < STEPS else zero8) + pltpu.roll(into[k], 8, axis=1) for k in range(4)]
    square = jnp.concatenate(parts + [jnp.zeros((96, 128), F32)], axis=0)
    mix = square.T[0:16, :]
    high = rounded(mix)
    mix = (high + pltpu.roll(high, 32, axis=1) + pltpu.roll(mix - high, 64, axis=1)).astype(BF16)[:, 0:96]

    def combined(r, a):
        cols = [
            jnp.concatenate([X[k, pl.ds((a + b) * ROWS + r, NV, stride=BLK), :] for k in range(4)], axis=0)
            for b in range(2)
        ]
        wide = jnp.concatenate(cols, axis=1)
        high = rounded(wide)
        stacked = jnp.concatenate([high, wide - high, high], axis=0).astype(BF16)
        return jnp.dot(mix, stacked, preferred_element_type=F32)

    def finish(r, c):
        for a in (0, 2):
            out = combined(r, a)
            for b in range(2):
                o_sc[pl.ds(r * AZL + a + b, NV, stride=RC * AZL), :] = out[0:8, b * 128 : b * 128 + 128]
                o_rc[pl.ds(r * AZL + a + b, NV, stride=RC * AZL), :] = out[8:16, b * 128 : b * 128 + 128]
        return c

    lax.fori_loop(0, RC, finish, 0, unroll=4)

    def finish_shell(r, c):
        for a in (0, 2):
            out = combined(RC + r, a)
            for b in range(2):
                o_ss[pl.ds(r * AZL + a + b, NV, stride=RS * AZL), :] = out[0:8, b * 128 : b * 128 + 128]
                o_rs[pl.ds(r * AZL + a + b, NV, stride=RS * AZL), :] = out[8:16, b * 128 : b * 128 + 128]
        return c

    lax.fori_loop(0, RS, finish_shell, 0, unroll=2)

    stores = [
        pltpu.make_async_copy(src, dst, out_sem.at[i])
        for i, (src, dst) in enumerate([(o_sc, sol_c), (o_rc, res_c), (o_ss, sol_s), (o_rs, res_s)])
    ]
    for store in stores:
        store.start()
    for k in range(STEPS):
        sent(k)
    for store in stores:
        store.wait()


def per_device(cavity_block, shell_block, column_matrix, shell_matrix, shifted_diagonal, shell_diagonal, wet_area):
    nc, ns = NV * RC * AZL, NV * RS * AZL
    anywhere = pl.BlockSpec(memory_space=pl.ANY)
    outs = pl.pallas_call(
        kernel,
        out_shape=(
            jax.ShapeDtypeStruct((nc, 128), F32),
            jax.ShapeDtypeStruct((nc, 128), F32),
            jax.ShapeDtypeStruct((ns, 128), F32),
            jax.ShapeDtypeStruct((ns, 128), F32),
        ),
        in_specs=[anywhere] * 7,
        out_specs=(anywhere,) * 4,
        scratch_shapes=[
            pltpu.VMEM((4, NV * BLK, 128), F32),
            pltpu.VMEM((STEPS, NV, ROWS, 128), F32),
            pltpu.VMEM((STEPS, NV, ROWS, 128), F32),
            pltpu.VMEM((STEPS, NV, BLK, 128), F32),
            pltpu.VMEM((STEPS, NV, 8, 128), F32),
            pltpu.VMEM((STEPS, NV, 8, 128), F32),
            pltpu.VMEM((AZL, ROWS, 128), F32),
            pltpu.VMEM((64, 256), BF16),
            pltpu.VMEM((64, 128), F32),
            pltpu.VMEM((128, 128), F32),
            pltpu.VMEM((16, 8, 128), F32),
            pltpu.VMEM((16, 8, 128), F32),
            pltpu.VMEM((nc, 128), F32),
            pltpu.VMEM((ns, 128), F32),
            pltpu.VMEM((RC * AZL, 128), F32),
            pltpu.VMEM((RS * AZL, 128), F32),
            pltpu.VMEM((AZL, 128), F32),
            pltpu.VMEM((RC, RC), F32),
            pltpu.VMEM((RS, RS), F32),
            pltpu.VMEM((nc, 128), F32),
            pltpu.VMEM((nc, 128), F32),
            pltpu.VMEM((ns, 128), F32),
            pltpu.VMEM((ns, 128), F32),
            pltpu.SemaphoreType.DMA((7,)),
            pltpu.SemaphoreType.DMA((4,)),
            pltpu.SemaphoreType.DMA((STEPS, 4)),
            pltpu.SemaphoreType.DMA((STEPS, NV, 4)),
            pltpu.SemaphoreType.DMA((16,)),
            pltpu.SemaphoreType.DMA((16,)),
            pltpu.SemaphoreType.DMA((16,)),
            pltpu.SemaphoreType.DMA((16,)),
        ],
        compiler_params=pltpu.CompilerParams(
            collective_id=0, has_side_effects=True, vmem_limit_bytes=32 * 1024 * 1024
        ),
        name="block_cg",
    )(
        cavity_block.reshape(nc, 128),
        shell_block.reshape(ns, 128),
        column_matrix.reshape(RC, RC),
        shell_matrix,
        shifted_diagonal.reshape(RC * AZL, 128),
        shell_diagonal.reshape(RS * AZL, 128),
        wet_area,
    )
    return (
        outs[0].reshape(NV, RC, AZL, 128),
        outs[1].reshape(NV, RC, AZL, 128),
        outs[2].reshape(NV, RS, AZL, 128),
        outs[3].reshape(NV, RS, AZL, 128),
    )


def solution(mesh):
    return jax.shard_map(
        per_device,
        mesh=mesh,
        in_specs=(
            P(None, "grp", "az", "ax"),
            P(None, None, "az", "ax"),
            P("grp", None, None),
            P(),
            P("grp", "az", "ax"),
            P(None, "az", "ax"),
            P("az", "ax"),
        ),
        out_specs=(
            P(None, "grp", "az", "ax"),
            P(None, "grp", "az", "ax"),
            P(None, None, "az", "ax"),
            P(None, None, "az", "ax"),
        ),
        check_vma=False,
    )
```

profile of v0, /device:TPU:1, one launch (start us, length us, event | category | flops | bytes accessed | tf_op | source)
XLA Modules:
  0.0 63.7 jit_solution(11589186829532126531)
XLA Ops:
  0.6 0.0 copy-start.5
  0.6 0.0 copy-start.6
  0.7 0.7 %copy-done.5 = f32[6,6]{1,0:T(8,128)S(1)} copy-done((f32[6,6]{1,0:T(8,128)S(1)}, f32[6,6]{1,0:T(8,128)}, u32[]{:S(2)}) %copy-start.5) | copy-done | bytes 168
  1.3 0.0 copy-done.6
  1.3 0.0 copy-start
  1.3 1.1 %copy-done = f32[8,48,4,128]{3,2,1,0:T(4,128)S(1)} copy-done((f32[8,48,4,128]{3,2,1,0:T(4,128)S(1)}, f32[8,48,4,128]{3,2,1,0:T(4,128)}, u32[]{:S(2)}) %copy-start) | copy-done | bytes 786456
  2.5 0.0 copy-start.1
  2.5 0.9 %copy-done.1 = f32[8,6,4,128]{3,2,1,0:T(4,128)S(1)} copy-done((f32[8,6,4,128]{3,2,1,0:T(4,128)S(1)}, f32[8,6,4,128]{3,2,1,0:T(4,128)}, u32[]{:S(2)}) %copy-start.1) | copy-done | bytes 98328
  3.4 0.0 copy-start.2
  3.4 0.9 %copy-done.2 = f32[48,4,128]{2,1,0:T(4,128)S(1)} copy-done((f32[48,4,128]{2,1,0:T(4,128)S(1)}, f32[48,4,128]{2,1,0:T(4,128)}, u32[]{:S(2)}) %copy-start.2) | copy-done | bytes 98328
  4.3 0.0 copy-start.3
  4.3 0.7 %copy-done.3 = f32[1,48,48]{2,1,0:T(8,128)S(1)} copy-done((f32[1,48,48]{2,1,0:T(8,128)S(1)}, f32[1,48,48]{2,1,0:T(8,128)}, u32[]{:S(2)}) %copy-start.3) | copy-done | bytes 9240
  5.0 0.0 copy-start.4
  5.0 0.7 %copy-done.4 = f32[6,4,128]{2,1,0:T(4,128)S(1)} copy-done((f32[6,4,128]{2,1,0:T(4,128)S(1)}, f32[6,4,128]{2,1,0:T(4,128)}, u32[]{:S(2)}) %copy-start.4) | copy-done | bytes 12312
  5.7 55.0 %block_cg.1 = (f32[1536,128]{1,0:T(8,128)S(1)}, f32[1536,128]{1,0:T(8,128)S(1)}, f32[192,128]{1,0:T(8,128)S(1)}, f32[192,128]{1,0:T(8,128)S(1)}) custom-call(f32[1536,128]{1,0:T(8,128)S(1)} %bitcast.11, f32[192,128]{1,0:T(8,128)S(1)} %bitcast.14, f32[48,48]{1,0:T(8,128)S(1)} %bitcast.16, f32[6,6]{1,0:T(8,128)S(1)} %copy-done.5, f32[192,128]{1,0:T(8,128)S(1)} %bitcast.15, ...), custom_call_target="tpu_custom_call" | custom-call | tf_op jit(solution)/shard_map/block_cg/pallas_call | solution.py:347
  60.7 0.9 %copy.15 = f32[8,48,4,128]{3,2,1,0:T(4,128)} copy(f32[8,48,4,128]{3,2,1,0:T(4,128)S(1)} %bitcast.10) | data formatting | bytes 1572864
  61.6 0.9 %copy.16 = f32[8,48,4,128]{3,2,1,0:T(4,128)} copy(f32[8,48,4,128]{3,2,1,0:T(4,128)S(1)} %bitcast.9) | data formatting | bytes 1572864
  62.5 0.6 %copy.17 = f32[8,6,4,128]{3,2,1,0:T(4,128)} copy(f32[8,6,4,128]{3,2,1,0:T(4,128)S(1)} %bitcast.13) | data formatting | bytes 196608
  63.1 0.6 %copy.18 = f32[8,6,4,128]{3,2,1,0:T(4,128)} copy(f32[8,6,4,128]{3,2,1,0:T(4,128)S(1)} %bitcast.12) | data formatting | bytes 196608
Async XLA Ops:
  0.6 0.7 %copy-start.5 = (f32[6,6]{1,0:T(8,128)S(1)}, f32[6,6]{1,0:T(8,128)}, u32[]{:S(2)}) copy-start(f32[6,6]{1,0:T(8,128)} %shm.1) | copy-start | bytes 436
  0.6 0.7 %copy-start.6 = (f32[4,128]{1,0:T(4,128)S(1)}, f32[4,128]{1,0:T(4,128)}, u32[]{:S(2)}) copy-start(f32[4,128]{1,0:T(4,128)} %wet.1) | copy-start | bytes 6148
  1.3 1.1 %copy-start = (f32[8,48,4,128]{3,2,1,0:T(4,128)S(1)}, f32[8,48,4,128]{3,2,1,0:T(4,128)}, u32[]{:S(2)}) copy-start(f32[8,48,4,128]{3,2,1,0:T(4,128)} %param.7) | copy-start | bytes 2359300
  2.5 0.9 %copy-start.1 = (f32[8,6,4,128]{3,2,1,0:T(4,128)S(1)}, f32[8,6,4,128]{3,2,1,0:T(4,128)}, u32[]{:S(2)}) copy-start(f32[8,6,4,128]{3,2,1,0:T(4,128)} %param.8) | copy-start | bytes 294916
  3.4 0.9 %copy-start.2 = (f32[48,4,128]{2,1,0:T(4,128)S(1)}, f32[48,4,128]{2,1,0:T(4,128)}, u32[]{:S(2)}) copy-start(f32[48,4,128]{2,1,0:T(4,128)} %param.11) | copy-start | bytes 294916
  4.3 0.7 %copy-start.3 = (f32[1,48,48]{2,1,0:T(8,128)S(1)}, f32[1,48,48]{2,1,0:T(8,128)}, u32[]{:S(2)}) copy-start(f32[1,48,48]{2,1,0:T(8,128)} %param.9) | copy-start | bytes 27652
  5.0 0.7 %copy-start.4 = (f32[6,4,128]{2,1,0:T(4,128)S(1)}, f32[6,4,128]{2,1,0:T(4,128)}, u32[]{:S(2)}) copy-start(f32[6,4,128]{2,1,0:T(4,128)} %param.12) | copy-start | bytes 36868
where the time goes:
time: 64.1 us; the launch traced here: 63.7 us
  Pallas kernels  55 us (86%)
  local copies, waits for them, and re-layouts  8.08 us (13%)
  between operations  0.66 us (1%)
    pallas_call x1, Pallas kernels, per_device(): pl.pallas_call(kernel, out_shape=(jax.ShapeDtypeStruct((nc, 128), F32), j...  55 us
    unnamed x18, local copies, waits for them, and re-layouts  8.08 us

commit v1 on v0

--- a/solution.py
+++ b/solution.py
@@ -24,11 +24,10 @@
 
 def kernel(
     cav, shl, colm, shm, dia, sdia, wet,
-    sol_c, res_c, sol_s, res_s,
-    X, HL, HR, SB, IS, IR, DG, W, STG, ACC, RX1, RX2,
+    X, MIX,
+    HL, HR, SB, IS, IR, DG, W, STG, ACC, RX1, RX2,
     raw_c, raw_s, raw_d, raw_sd, raw_w, raw_cm, raw_sm,
-    o_sc, o_rc, o_ss, o_rs,
-    in_sem, out_sem, send_sem, recv_sem, s1, r1, s2, r2,
+    in_sem, send_sem, recv_sem, s1, r1, s2, r2,
 ):
     grp = lax.axis_index("grp")
     az = lax.axis_index("az")
@@ -297,7 +296,16 @@
     square = jnp.concatenate(parts + [jnp.zeros((96, 128), F32)], axis=0)
     mix = square.T[0:16, :]
     high = rounded(mix)
-    mix = (high + pltpu.roll(high, 32, axis=1) + pltpu.roll(mix - high, 64, axis=1)).astype(BF16)[:, 0:96]
+    MIX[...] = high + pltpu.roll(high, 32, axis=1) + pltpu.roll(mix - high, 64, axis=1)
+    for k in range(STEPS):
+        sent(k)
+
+
+PIECES = 4
+
+
+def finish_kernel(X, MIX, sol_c, res_c, sol_s, res_s, o_sc, o_rc, o_ss, o_rs, sem):
+    mix = MIX[...].astype(BF16)[:, 0:96]
 
     def combined(r, a):
         cols = [
@@ -309,53 +317,63 @@
         stacked = jnp.concatenate([high, wide - high, high], axis=0).astype(BF16)
         return jnp.dot(mix, stacked, preferred_element_type=F32)
 
-    def finish(r, c):
-        for a in (0, 2):
-            out = combined(r, a)
-            for b in range(2):
-                o_sc[pl.ds(r * AZL + a + b, NV, stride=RC * AZL), :] = out[0:8, b * 128 : b * 128 + 128]
-                o_rc[pl.ds(r * AZL + a + b, NV, stride=RC * AZL), :] = out[8:16, b * 128 : b * 128 + 128]
-        return c
-
-    lax.fori_loop(0, RC, finish, 0, unroll=4)
-
-    def finish_shell(r, c):
-        for a in (0, 2):
-            out = combined(RC + r, a)
-            for b in range(2):
-                o_ss[pl.ds(r * AZL + a + b, NV, stride=RS * AZL), :] = out[0:8, b * 128 : b * 128 + 128]
-                o_rs[pl.ds(r * AZL + a + b, NV, stride=RS * AZL), :] = out[8:16, b * 128 : b * 128 + 128]
-        return c
-
-    lax.fori_loop(0, RS, finish_shell, 0, unroll=2)
-
-    stores = [
-        pltpu.make_async_copy(src, dst, out_sem.at[i])
-        for i, (src, dst) in enumerate([(o_sc, sol_c), (o_rc, res_c), (o_ss, sol_s), (o_rs, res_s)])
+    def rows_of(first, rows, o_sol, o_res):
+        def body(r, c):
+            for a in (0, 2):
+                out = combined(first + r, a)
+                for b in range(2):
+                    here = pl.ds(r * AZL + a + b, NV, stride=rows * AZL)
+                    o_sol[here, :] = out[0:8, b * 128 : b * 128 + 128]
+                    o_res[here, :] = out[8:16, b * 128 : b * 128 + 128]
+            return c
+
+        return body
+
+    def piece(i, o, dst, slot, rows):
+        copies = []
+        for v in range(NV):
+            here = pl.ds(v * RC * AZL + i * rows, rows)
+            copies.append(pltpu.make_async_copy(o.at[here, :], dst.at[here, :], sem.at[slot]))
+        return copies
+
+    each = RC // PIECES
+    lax.fori_loop(0, RS, rows_of(RC, RS, o_ss, o_rs), 0, unroll=2)
+    small = [
+        pltpu.make_async_copy(o_ss, sol_s, sem.at[2]),
+        pltpu.make_async_copy(o_rs, res_s, sem.at[3]),
     ]
-    for store in stores:
-        store.start()
-    for k in range(STEPS):
-        sent(k)
-    for store in stores:
-        store.wait()
+    for copy in small:
+        copy.start()
+    for i in range(PIECES):
+        lax.fori_loop(i * each, (i + 1) * each, rows_of(0, RC, o_sc, o_rc), 0, unroll=4)
+        for copy in piece(i, o_sc, sol_c, 0, each * AZL) + piece(i, o_rc, res_c, 1, each * AZL):
+            copy.start()
+    for copy in small:
+        copy.wait()
+    pltpu.make_async_copy(o_sc, sol_c, sem.at[0]).wait()
+    pltpu.make_async_copy(o_rc, res_c, sem.at[1]).wait()
 
 
 def per_device(cavity_block, shell_block, column_matrix, shell_matrix, shifted_diagonal, shell_diagonal, wet_area):
     nc, ns = NV * RC * AZL, NV * RS * AZL
     anywhere = pl.BlockSpec(memory_space=pl.ANY)
-    outs = pl.pallas_call(
+    args = (
+        cavity_block.reshape(nc, 128),
+        shell_block.reshape(ns, 128),
+        column_matrix.reshape(RC, RC),
+        shell_matrix,
+        shifted_diagonal.reshape(RC * AZL, 128),
+        shell_diagonal.reshape(RS * AZL, 128),
+        wet_area,
+    )
+    args = [pltpu.with_memory_space_constraint(x, pltpu.HBM) for x in args]
+    inside = pl.BlockSpec(memory_space=pltpu.VMEM)
+    basis, mix = pl.pallas_call(
         kernel,
-        out_shape=(
-            jax.ShapeDtypeStruct((nc, 128), F32),
-            jax.ShapeDtypeStruct((nc, 128), F32),
-            jax.ShapeDtypeStruct((ns, 128), F32),
-            jax.ShapeDtypeStruct((ns, 128), F32),
-        ),
+        out_shape=(pltpu.VMEM((4, NV * BLK, 128), F32), pltpu.VMEM((16, 128), F32)),
         in_specs=[anywhere] * 7,
-        out_specs=(anywhere,) * 4,
+        out_specs=(inside, inside),
         scratch_shapes=[
-            pltpu.VMEM((4, NV * BLK, 128), F32),
             pltpu.VMEM((STEPS, NV, ROWS, 128), F32),
             pltpu.VMEM((STEPS, NV, ROWS, 128), F32),
             pltpu.VMEM((STEPS, NV, BLK, 128), F32),
@@ -374,12 +392,7 @@
             pltpu.VMEM((AZL, 128), F32),
             pltpu.VMEM((RC, RC), F32),
             pltpu.VMEM((RS, RS), F32),
-            pltpu.VMEM((nc, 128), F32),
-            pltpu.VMEM((nc, 128), F32),
-            pltpu.VMEM((ns, 128), F32),
-            pltpu.VMEM((ns, 128), F32),
             pltpu.SemaphoreType.DMA((7,)),
-            pltpu.SemaphoreType.DMA((4,)),
             pltpu.SemaphoreType.DMA((STEPS, 4)),
             pltpu.SemaphoreType.DMA((STEPS, NV, 4)),
             pltpu.SemaphoreType.DMA((16,)),
@@ -388,17 +401,32 @@
             pltpu.SemaphoreType.DMA((16,)),
         ],
         compiler_params=pltpu.CompilerParams(
-            collective_id=0, has_side_effects=True, vmem_limit_bytes=32 * 1024 * 1024
+            collective_id=0, has_side_effects=True, vmem_limit_bytes=24 * 1024 * 1024
         ),
         name="block_cg",
+    )(*args)
+    outs = pl.pallas_call(
+        finish_kernel,
+        out_shape=(
+            jax.ShapeDtypeStruct((nc, 128), F32),
+            jax.ShapeDtypeStruct((nc, 128), F32),
+            jax.ShapeDtypeStruct((ns, 128), F32),
+            jax.ShapeDtypeStruct((ns, 128), F32),
+        ),
+        in_specs=[inside, inside],
+        out_specs=(anywhere,) * 4,
+        scratch_shapes=[
+            pltpu.VMEM((nc, 128), F32),
+            pltpu.VMEM((nc, 128), F32),
+            pltpu.VMEM((ns, 128), F32),
+            pltpu.VMEM((ns, 128), F32),
+            pltpu.SemaphoreType.DMA((4,)),
+        ],
+        compiler_params=pltpu.CompilerParams(vmem_limit_bytes=24 * 1024 * 1024),
+        name="combine_basis",
     )(
-        cavity_block.reshape(nc, 128),
-        shell_block.reshape(ns, 128),
-        column_matrix.reshape(RC, RC),
-        shell_matrix,
-        shifted_diagonal.reshape(RC * AZL, 128),
-        shell_diagonal.reshape(RS * AZL, 128),
-        wet_area,
+        pltpu.with_memory_space_constraint(basis, pltpu.VMEM),
+        pltpu.with_memory_space_constraint(mix, pltpu.VMEM),
     )
     return (
         outs[0].reshape(NV, RC, AZL, 128),

time: 64.1 us -> 55.9 us (0.87)
  local copies, waits for them, and re-layouts: 8.08 us -> 0 us
    unnamed x18 -> x0, local copies, waits for them, and re-layouts: 8.08 us -> none
    pallas_call x1 -> x2, Pallas kernels: 55 us -> 55.2 us  [the longest x1 50.4 us: per_device(): pl.pallas_call(kernel, out_shape=(pltpu.VMEM((4, NV * BLK, 128), F32), pl...]
where the time goes in v1:
time: 55.9 us; the launch traced here: 55.8 us
  Pallas kernels  55.2 us (99%)
  between operations  0.64 us (1%)
    pallas_call x1, Pallas kernels, per_device(): pl.pallas_call(kernel, out_shape=(pltpu.VMEM((4, NV * BLK, 128), F32), pl...  50.4 us
    pallas_call x1, Pallas kernels, per_device(): pl.pallas_call(finish_kernel, out_shape=(jax.ShapeDtypeStruct((nc, 128),...  4.75 us

profile of v1, /device:TPU:1, one launch (start us, length us, event | category | flops | bytes accessed | tf_op | source)
XLA Modules:
  0.0 55.8 jit_solution(13177090963021319746)
XLA Ops:
  0.6 50.4 %block_cg.1 = (f32[4,1792,128]{2,1,0:T(8,128)S(1)}, f32[16,128]{1,0:T(8,128)S(1)}) custom-call(f32[1536,128]{1,0:T(8,128)} %bitcast.9, f32[192,128]{1,0:T(8,128)} %bitcast.10, f32[48,48]{1,0:T(8,128)} %bitcast.12, f32[6,6]{1,0:T(8,128)} %shm.1, f32[192,128]{1,0:T(8,128)} %bitcast.11, f32[24,128]{1,0:T(8,128)} %bitcast.13, f32[4,128]{1,0:T(4,128)} %wet.1), custom_call_target="tpu_custom_call" | custom-call | tf_op jit(solution)/shard_map/block_cg/pallas_call | solution.py:371
  51.0 4.8 %combine_basis.1 = (f32[1536,128]{1,0:T(8,128)}, f32[1536,128]{1,0:T(8,128)}, f32[192,128]{1,0:T(8,128)}, f32[192,128]{1,0:T(8,128)}) custom-call(f32[4,1792,128]{2,1,0:T(8,128)S(1)} %get-tuple-element.10.X, f32[16,128]{1,0:T(8,128)S(1)} %get-tuple-element.11.MIX), custom_call_target="tpu_custom_call" | custom-call | tf_op jit(solution)/shard_map/combine_basis/pallas_call | solution.py:408

commit v2 on v1

--- a/solution.py
+++ b/solution.py
@@ -24,10 +24,10 @@
 
 def kernel(
     cav, shl, colm, shm, dia, sdia, wet,
-    X, MIX,
-    HL, HR, SB, IS, IR, DG, W, STG, ACC, RX1, RX2,
+    T, MIX,
+    X, HL, HR, SB, IS, IR, WS, WR, DG, W, STG, ACC, RX,
     raw_c, raw_s, raw_d, raw_sd, raw_w, raw_cm, raw_sm,
-    in_sem, send_sem, recv_sem, s1, r1, s2, r2,
+    in_sem, send_sem, recv_sem, sum_send, sum_recv,
 ):
     grp = lax.axis_index("grp")
     az = lax.axis_index("az")
@@ -83,28 +83,13 @@
     lane = lax.broadcasted_iota(jnp.int32, (8, 128), 1)
     row = lax.broadcasted_iota(jnp.int32, (8, 128), 0)
 
-    for load in loads:
-        load.wait()
-
-    def place(v, c):
-        for a in range(AZL):
-            at = v * BLK + a * ROWS
-            X[0, pl.ds(pl.multiple_of(at, 8), RC), :] = raw_c[pl.ds(v * (RC * AZL) + a, RC, stride=AZL), :]
-            tail = jnp.concatenate(
-                [raw_s[pl.ds(v * (RS * AZL) + a, RS, stride=AZL), :], jnp.zeros((2, 128), F32)], axis=0
-            )
-            X[0, pl.ds(pl.multiple_of(at + RC, 8), 8), :] = tail
-        return c
-
-    lax.fori_loop(0, NV, place, 0)
-
     def rows_to_send(k, v):
         for a in range(AZL):
             at = v * BLK + a * ROWS
             first = X[k, pl.ds(pl.multiple_of(at, 8), 8), :][0:1]
             last = X[k, pl.ds(pl.multiple_of(at + 40, 8), 8), :][7:8]
             IS[k, v, a : a + 1, :] = jnp.where(is_outer, first, last)
-            IS[k, v, 4 + a : 5 + a, :] = last
+            WS[k, v, a : a + 1, :] = last
 
     def exchange(k, v):
         base = pl.multiple_of(v * BLK, 8)
@@ -128,21 +113,52 @@
             ),
         )
 
+    def wall_copy(k, v):
+        return pltpu.make_async_remote_copy(
+            WS.at[k, v], WR.at[k, v], send_sem.at[k, 4], recv_sem.at[k, v, 4], device_id=to_half, device_id_type=MESH
+        )
+
+    def send(k, v):
+        rows_to_send(k, v)
+        for copy in exchange(k, v):
+            copy.start()
+
+        @pl.when(is_outer)
+        def _():
+            wall_copy(k, v).start()
+
     def sent(k):
-        for i, (buf, where) in enumerate(((HL, to_right), (HR, to_left), (SB, to_core), (IS, to_half))):
+        def all_of(i, buf, where):
             pltpu.make_async_remote_copy(
                 buf.at[k], buf.at[k], send_sem.at[k, i], recv_sem.at[k, 0, i], device_id=where, device_id_type=MESH
             ).wait_send()
 
+        for i, (buf, where) in enumerate(((HL, to_right), (HR, to_left), (SB, to_core), (IS, to_half))):
+            all_of(i, buf, where)
+
+        @pl.when(is_outer)
+        def _():
+            all_of(4, WS, to_half)
+
     pl.semaphore_wait(barrier, 34)
 
+    for load in loads[:2]:
+        load.wait()
+
     def first_send(v, c):
-        rows_to_send(0, v)
-        for copy in exchange(0, v):
-            copy.start()
+        for a in range(AZL):
+            at = v * BLK + a * ROWS
+            X[0, pl.ds(pl.multiple_of(at, 8), RC), :] = raw_c[pl.ds(v * (RC * AZL) + a, RC, stride=AZL), :]
+            tail = jnp.concatenate(
+                [raw_s[pl.ds(v * (RS * AZL) + a, RS, stride=AZL), :], jnp.zeros((2, 128), F32)], axis=0
+            )
+            X[0, pl.ds(pl.multiple_of(at + RC, 8), 8), :] = tail
+        send(0, v)
         return c
 
     lax.fori_loop(0, NV, first_send, 0)
+    for load in loads[2:]:
+        load.wait()
 
     for a in range(AZL):
         DG[a, 0:RC, :] = raw_d[pl.ds(a, RC, stride=AZL), :] + (4.0 - THETA)
@@ -177,12 +193,17 @@
             base = v * BLK
             for copy in exchange(k, v):
                 copy.wait_recv()
+
+            @pl.when(grp == 0)
+            def _():
+                wall_copy(k, v).wait_recv()
+
             own = [X[k, pl.ds(pl.multiple_of(base + a * ROWS, 8), ROWS), :] for a in range(AZL)]
-            got = IR[k, v]
+            got, far = IR[k, v], WR[k, v]
             spread = []
             for a in range(AZL):
                 wet_row = raw_w[a : a + 1, :]
-                wall = jnp.where(is_outer, own[a][RC - 1 : RC], got[4 + a : 5 + a])
+                wall = jnp.where(is_outer, own[a][RC - 1 : RC], far[a : a + 1])
                 skin = own[a][RC : RC + 1]
                 extra = jnp.where(row == 0, got[a : a + 1], 0.0)
                 extra = jnp.where(row == 1, wet_row * wall, extra)
@@ -202,72 +223,100 @@
                 new = new - ((before + after) + (lower + upper))
                 X[k + 1, pl.ds(pl.multiple_of(base + a * ROWS, 8), ROWS), :] = new
             if k + 1 < STEPS:
-                rows_to_send(k + 1, v)
-                for copy in exchange(k + 1, v):
-                    copy.start()
-            even = [jnp.zeros((8, 128), F32) for _ in range(NV)]
-            odd = [jnp.zeros((8, 128), F32) for _ in range(NV)]
-            for p in range(BLK // 8):
-                here = pl.ds(pl.multiple_of(base + p * 8, 8), 8)
-                old, new = X[k, here, :], X[k + 1, here, :]
-                if p % 7 == 6:
-                    old, new = old * share, new * share
-                for w in range(NV):
-                    other = X[k, w * BLK + p * 8 : w * BLK + p * 8 + 8, :]
-                    even[w] += other * old
-                    odd[w] += other * new
+                send(k + 1, v)
+                which = [(k, k, 16 * k), (k, k + 1, 16 * k + 8)]
+            else:
+                which = [(k, k + 1, 16)]
+            return products(which, v, moments)
+
+        return body
+
+    def products(which, v, moments):
+        k = which[0][0]
+        base = v * BLK
+        sums = [[jnp.zeros((8, 128), F32) for _ in range(NV)] for _ in which]
+        for p in range(BLK // 8):
+            here = pl.ds(pl.multiple_of(base + p * 8, 8), 8)
+            mine = [X[j, here, :] for _, j, _ in which]
+            if p % 7 == 6:
+                mine = [m * share for m in mine]
             for w in range(NV):
-                ACC[w * 8 : w * 8 + 8, :] = even[w]
-                ACC[64 + w * 8 : 72 + w * 8, :] = odd[w]
-            for half in range(2):
-                total = ACC[pl.ds(64 * half, 8, stride=8), :]
-                for s in range(1, 8):
-                    total += ACC[pl.ds(64 * half + s, 8, stride=8), :]
-                total = jnp.sum(total, axis=1, keepdims=True)
-                moments = jnp.where(lane == 8 * (2 * k + half) + v, total, moments)
-            return moments
-
-        return body
-
-    moments = jnp.zeros((8, 128), F32)
-    for k in range(STEPS):
-        moments = lax.fori_loop(0, NV, apply(k), moments)
-
-    def total_of(value, me, peer, buf, ssem, rsem):
-        buf[me] = value
-
-        def copy_of(d):
-            s, where = peer(d)
-            return s, pltpu.make_async_remote_copy(
-                buf.at[me], buf.at[me], ssem.at[d], rsem.at[me], device_id=where, device_id_type=MESH
-            )
+                other = X[k, w * BLK + p * 8 : w * BLK + p * 8 + 8, :]
+                for q in range(len(which)):
+                    sums[q][w] += other * mine[q]
+        for q, (_, _, at) in enumerate(which):
+            for w in range(NV):
+                ACC[64 * q + w * 8 : 64 * q + w * 8 + 8, :] = sums[q][w]
+            total = ACC[pl.ds(64 * q, 8, stride=8), :]
+            for s in range(1, 8):
+                total += ACC[pl.ds(64 * q + s, 8, stride=8), :]
+            total = jnp.sum(total, axis=1, keepdims=True)
+            moments = jnp.where(lane == at + v, total, moments)
+        return moments
+
+    def copy_of(i, d):
+        me, (s, where) = (me1, peer1(d)) if i % 2 == 0 else (me2, peer2(d))
+        out = pltpu.make_async_remote_copy(
+            RX.at[i, me], RX.at[i, me], sum_send.at[i, d], sum_recv.at[i, me], device_id=where, device_id_type=MESH
+        )
+        back = pltpu.make_async_remote_copy(
+            RX.at[i, s], RX.at[i, s], sum_send.at[i, d], sum_recv.at[i, s], device_id=where, device_id_type=MESH
+        )
+        return out, back
+
+    def sum_start(i, value):
+        RX[i, me1 if i % 2 == 0 else me2] = value
 
         def start(d, c):
-            copy_of(d)[1].start()
+            copy_of(i, d)[0].start()
             return c
 
+        lax.fori_loop(1, 16, start, 0)
+
+    def sum_finish(i):
         def wait(d, c):
-            s, where = peer(d)
-            pltpu.make_async_remote_copy(
-                buf.at[s], buf.at[s], ssem.at[d], rsem.at[s], device_id=where, device_id_type=MESH
-            ).wait_recv()
+            copy_of(i, d)[1].wait_recv()
             return c
 
+        lax.fori_loop(1, 16, wait, 0)
+        result = RX[i, 0]
+        for s in range(1, 16):
+            result += RX[i, s]
+        return result
+
+    def sum_drain(i):
         def drain(d, c):
-            copy_of(d)[1].wait_send()
+            copy_of(i, d)[0].wait_send()
             return c
 
-        lax.fori_loop(1, 16, start, 0)
-        lax.fori_loop(1, 16, wait, 0)
-        result = buf[0]
-        for s in range(1, 16):
-            result += buf[s]
         lax.fori_loop(1, 16, drain, 0)
-        return result
-
-    gram = total_of(moments, me1, peer1, RX1, s1, r1)
-    gram = total_of(gram, me2, peer2, RX2, s2, r2)
-
+
+    def prepare(r, c):
+        for half in range(2):
+            cols = [
+                jnp.concatenate(
+                    [X[k, pl.ds((2 * half + b) * ROWS + r, NV, stride=BLK), :] for k in range(4)], axis=0
+                )
+                for b in range(2)
+            ]
+            wide = jnp.concatenate(cols, axis=1)
+            high = rounded(wide)
+            T[2 * r + half] = jnp.concatenate([high, wide - high, high], axis=0).astype(BF16)
+        return c
+
+    zero8 = jnp.zeros((8, 128), F32)
+    early = lax.fori_loop(0, NV, apply(0), zero8)
+    early = lax.fori_loop(0, NV, apply(1), early)
+    early = lax.fori_loop(0, NV, lambda v, m: products([(2, 2, 32)], v, m), early)
+    sum_start(0, early)
+    late = lax.fori_loop(0, NV, apply(2), zero8)
+    sum_start(2, late)
+    early = sum_finish(0)
+    sum_start(1, early)
+    lax.fori_loop(0, 27, prepare, 0, unroll=3)
+    late = sum_finish(2)
+    sum_start(3, late)
+    gram = sum_finish(1)
     shifted = pltpu.roll(gram, 120, axis=1) + THETA * gram
     table = []
     for i in range(STEPS):
@@ -276,6 +325,9 @@
         table.append(jnp.where(lane < 24, left_part, jnp.where(lane < 32, right_part, 0.0)))
     for p in range(8 * STEPS):
         at, r = p // 8, p % 8
+        if p == 16:
+            lax.fori_loop(27, 54, prepare, 0, unroll=3)
+            table[2] = table[2] + sum_finish(3)
         pivot_row = table[at][r : r + 1, :]
         scaled = pivot_row * (1.0 / pivot_row[:, p : p + 1])
         for i in range(STEPS):
@@ -291,7 +343,6 @@
         -(y[1] + THETA * y[2]),
         -y[2],
     ]
-    zero8 = jnp.zeros((8, 128), F32)
     parts = [(y[k] if k < STEPS else zero8) + pltpu.roll(into[k], 8, axis=1) for k in range(4)]
     square = jnp.concatenate(parts + [jnp.zeros((96, 128), F32)], axis=0)
     mix = square.T[0:16, :]
@@ -299,28 +350,20 @@
     MIX[...] = high + pltpu.roll(high, 32, axis=1) + pltpu.roll(mix - high, 64, axis=1)
     for k in range(STEPS):
         sent(k)
+    for i in range(4):
+        sum_drain(i)
 
 
 PIECES = 4
 
 
-def finish_kernel(X, MIX, sol_c, res_c, sol_s, res_s, o_sc, o_rc, o_ss, o_rs, sem):
+def finish_kernel(T, MIX, sol_c, res_c, sol_s, res_s, o_sc, o_rc, o_ss, o_rs, sem):
     mix = MIX[...].astype(BF16)[:, 0:96]
-
-    def combined(r, a):
-        cols = [
-            jnp.concatenate([X[k, pl.ds((a + b) * ROWS + r, NV, stride=BLK), :] for k in range(4)], axis=0)
-            for b in range(2)
-        ]
-        wide = jnp.concatenate(cols, axis=1)
-        high = rounded(wide)
-        stacked = jnp.concatenate([high, wide - high, high], axis=0).astype(BF16)
-        return jnp.dot(mix, stacked, preferred_element_type=F32)
 
     def rows_of(first, rows, o_sol, o_res):
         def body(r, c):
             for a in (0, 2):
-                out = combined(first + r, a)
+                out = jnp.dot(mix, T[2 * (first + r) + a // 2], preferred_element_type=F32)
                 for b in range(2):
                     here = pl.ds(r * AZL + a + b, NV, stride=rows * AZL)
                     o_sol[here, :] = out[0:8, b * 128 : b * 128 + 128]
@@ -370,21 +413,23 @@
     inside = pl.BlockSpec(memory_space=pltpu.VMEM)
     basis, mix = pl.pallas_call(
         kernel,
-        out_shape=(pltpu.VMEM((4, NV * BLK, 128), F32), pltpu.VMEM((16, 128), F32)),
+        out_shape=(pltpu.VMEM((2 * (RC + RS), 96, 256), BF16), pltpu.VMEM((16, 128), F32)),
         in_specs=[anywhere] * 7,
         out_specs=(inside, inside),
         scratch_shapes=[
+            pltpu.VMEM((4, NV * BLK, 128), F32),
             pltpu.VMEM((STEPS, NV, ROWS, 128), F32),
             pltpu.VMEM((STEPS, NV, ROWS, 128), F32),
             pltpu.VMEM((STEPS, NV, BLK, 128), F32),
-            pltpu.VMEM((STEPS, NV, 8, 128), F32),
-            pltpu.VMEM((STEPS, NV, 8, 128), F32),
+            pltpu.VMEM((STEPS, NV, AZL, 128), F32),
+            pltpu.VMEM((STEPS, NV, AZL, 128), F32),
+            pltpu.VMEM((STEPS, NV, AZL, 128), F32),
+            pltpu.VMEM((STEPS, NV, AZL, 128), F32),
             pltpu.VMEM((AZL, ROWS, 128), F32),
             pltpu.VMEM((64, 256), BF16),
             pltpu.VMEM((64, 128), F32),
             pltpu.VMEM((128, 128), F32),
-            pltpu.VMEM((16, 8, 128), F32),
-            pltpu.VMEM((16, 8, 128), F32),
+            pltpu.VMEM((4, 16, 8, 128), F32),
             pltpu.VMEM((nc, 128), F32),
             pltpu.VMEM((ns, 128), F32),
             pltpu.VMEM((RC * AZL, 128), F32),
@@ -393,15 +438,13 @@
             pltpu.VMEM((RC, RC), F32),
             pltpu.VMEM((RS, RS), F32),
             pltpu.SemaphoreType.DMA((7,)),
-            pltpu.SemaphoreType.DMA((STEPS, 4)),
-            pltpu.SemaphoreType.DMA((STEPS, NV, 4)),
-            pltpu.SemaphoreType.DMA((16,)),
-            pltpu.SemaphoreType.DMA((16,)),
-            pltpu.SemaphoreType.DMA((16,)),
-            pltpu.SemaphoreType.DMA((16,)),
+            pltpu.SemaphoreType.DMA((STEPS, 5)),
+            pltpu.SemaphoreType.DMA((STEPS, NV, 5)),
+            pltpu.SemaphoreType.DMA((4, 16)),
+            pltpu.SemaphoreType.DMA((4, 16)),
         ],
         compiler_params=pltpu.CompilerParams(
-            collective_id=0, has_side_effects=True, vmem_limit_bytes=24 * 1024 * 1024
+            collective_id=0, has_side_effects=True, vmem_limit_bytes=22 * 1024 * 1024
         ),
         name="block_cg",
     )(*args)
@@ -422,7 +465,7 @@
             pltpu.VMEM((ns, 128), F32),
             pltpu.SemaphoreType.DMA((4,)),
         ],
-        compiler_params=pltpu.CompilerParams(vmem_limit_bytes=24 * 1024 * 1024),
+        compiler_params=pltpu.CompilerParams(vmem_limit_bytes=22 * 1024 * 1024),
         name="combine_basis",
     )(
         pltpu.with_memory_space_constraint(basis, pltpu.VMEM),

time: 55.9 us -> 54.8 us (0.980)
  Pallas kernels: 55.2 us -> 54.1 us
    pallas_call x1, Pallas kernels: 4.75 us -> 3.63 us  [per_device(): pl.pallas_call(finish_kernel, out_shape=(jax.ShapeDtypeStruct((nc, 128),...]
where the time goes in v2:
time: 54.8 us; the launch traced here: 54.7 us
  Pallas kernels  54.1 us (99%)
  between operations  0.64 us (1%)
    pallas_call x1, Pallas kernels, per_device(): pl.pallas_call(kernel, out_shape=(pltpu.VMEM((2 * (RC + RS), 96, 256), BF...  50.5 us
    pallas_call x1, Pallas kernels, per_device(): pl.pallas_call(finish_kernel, out_shape=(jax.ShapeDtypeStruct((nc, 128),...  3.63 us

profile of v2, /device:TPU:1, one launch (start us, length us, event | category | flops | bytes accessed | tf_op | source)
XLA Modules:
  0.0 54.7 jit_solution(17579167097391171849)
XLA Ops:
  0.6 50.5 %block_cg.1 = (bf16[108,96,256]{2,1,0:T(8,128)(2,1)S(1)}, f32[16,128]{1,0:T(8,128)S(1)}) custom-call(f32[1536,128]{1,0:T(8,128)} %bitcast.9, f32[192,128]{1,0:T(8,128)} %bitcast.10, f32[48,48]{1,0:T(8,128)} %bitcast.12, f32[6,6]{1,0:T(8,128)} %shm.1, f32[192,128]{1,0:T(8,128)} %bitcast.11, f32[24,128]{1,0:T(8,128)} %bitcast.13, f32[4,128]{1,0:T(4,128)} %wet.1), custom_call_target="tpu_custom_call" | custom-call | tf_op jit(solution)/shard_map/block_cg/pallas_call | solution.py:414
  51.1 3.6 %combine_basis.1 = (f32[1536,128]{1,0:T(8,128)}, f32[1536,128]{1,0:T(8,128)}, f32[192,128]{1,0:T(8,128)}, f32[192,128]{1,0:T(8,128)}) custom-call(bf16[108,96,256]{2,1,0:T(8,128)(2,1)S(1)} %get-tuple-element.10.T, f32[16,128]{1,0:T(8,128)S(1)} %get-tuple-element.11.MIX), custom_call_target="tpu_custom_call" | custom-call | tf_op jit(solution)/shard_map/combine_basis/pallas_call | solution.py:451

commit v3 on v2

--- a/solution.py
+++ b/solution.py
@@ -9,6 +9,7 @@
 RC = 48
 RS = 6
 ROWS = 56
+LAYER = RC + RS
 AZL = 4
 BLK = AZL * ROWS
 STEPS = 3
@@ -27,7 +28,7 @@
     T, MIX,
     X, HL, HR, SB, IS, IR, WS, WR, DG, W, STG, ACC, RX,
     raw_c, raw_s, raw_d, raw_sd, raw_w, raw_cm, raw_sm,
-    in_sem, send_sem, recv_sem, sum_send, sum_recv,
+    in_sem, vec_sem, send_sem, recv_sem, sum_send, sum_recv,
 ):
     grp = lax.axis_index("grp")
     az = lax.axis_index("az")
@@ -42,10 +43,17 @@
     loads = [
         pltpu.make_async_copy(src, dst, in_sem.at[i])
         for i, (src, dst) in enumerate(
-            [(cav, raw_c), (shl, raw_s), (dia, raw_d), (sdia, raw_sd), (wet, raw_w), (colm, raw_cm), (shm, raw_sm)]
+            [(shl, raw_s), (dia, raw_d), (sdia, raw_sd), (wet, raw_w), (colm, raw_cm), (shm, raw_sm)]
         )
     ]
-    for load in loads:
+    def load_vector(v):
+        here = pl.ds(pl.multiple_of(v * (RC * AZL), 8), RC * AZL)
+        return pltpu.make_async_copy(cav.at[here, :], raw_c.at[here, :], vec_sem.at[v])
+
+    loads[0].start()
+    for v in range(NV):
+        load_vector(v).start()
+    for load in loads[1:]:
         load.start()
 
     barrier = pltpu.get_barrier_semaphore()
@@ -53,16 +61,21 @@
     def hello(where):
         pl.semaphore_signal(barrier, inc=1, device_id=where, device_id_type=MESH)
 
-    me1 = px * 4 + py
-    me2 = grp * 8 + pz * 2 + ax
-
-    def peer1(d):
-        s = lax.rem(me1 + d, 16)
-        return s, {"grp": grp, "az": (s // 4) * 16 + pz * 4 + lax.rem(s, 4), "ax": ax}
-
-    def peer2(d):
-        s = lax.rem(me2 + d, 16)
-        return s, {"grp": s // 8, "az": px * 16 + lax.rem(s // 2, 4) * 4 + py, "ax": lax.rem(s, 2)}
+    here1 = px * 4 + py
+    here2 = grp * 4 + pz
+    slots = (16, 8, 2)
+
+    def place_in(stage):
+        return (here1, here2, ax)[stage]
+
+    def peer(stage, d):
+        if stage == 0:
+            x, y = lax.rem(px + d // 4, 4), lax.rem(py + d % 4, 4)
+            return x * 4 + y, {"grp": grp, "az": x * 16 + pz * 4 + y, "ax": ax}
+        if stage == 1:
+            g, z = lax.rem(grp + d // 4, 2), lax.rem(pz + d % 4, 4)
+            return g * 4 + z, {"grp": g, "az": px * 16 + z * 4 + py, "ax": ax}
+        return 1 - ax, {"grp": grp, "az": az, "ax": 1 - ax}
 
     to_right = {"grp": grp, "az": right, "ax": ax}
     to_left = {"grp": grp, "az": left, "ax": ax}
@@ -71,12 +84,9 @@
     for where in (to_right, to_left, to_core, to_half):
         hello(where)
 
-    def hello_peers(d, c):
-        hello(peer1(d)[1])
-        hello(peer2(d)[1])
-        return c
-
-    lax.fori_loop(1, 16, hello_peers, 0)
+    for stage in range(2):
+        for d in range(1, slots[stage]):
+            hello(peer(stage, d)[1])
 
     outer = (grp == 1).astype(F32)
     is_outer = grp == 1
@@ -96,11 +106,11 @@
         top = pl.multiple_of(v * BLK + 3 * ROWS, 8)
         return (
             pltpu.make_async_remote_copy(
-                X.at[k, pl.ds(top, ROWS), :], HL.at[k, v], send_sem.at[k, 0], recv_sem.at[k, v, 0],
+                X.at[k, pl.ds(top, LAYER), :], HL.at[k, v, pl.ds(0, LAYER), :], send_sem.at[k, 0], recv_sem.at[k, v, 0],
                 device_id=to_right, device_id_type=MESH,
             ),
             pltpu.make_async_remote_copy(
-                X.at[k, pl.ds(base, ROWS), :], HR.at[k, v], send_sem.at[k, 1], recv_sem.at[k, v, 1],
+                X.at[k, pl.ds(base, LAYER), :], HR.at[k, v, pl.ds(0, LAYER), :], send_sem.at[k, 1], recv_sem.at[k, v, 1],
                 device_id=to_left, device_id_type=MESH,
             ),
             pltpu.make_async_remote_copy(
@@ -134,18 +144,26 @@
             ).wait_send()
 
         for i, (buf, where) in enumerate(((HL, to_right), (HR, to_left), (SB, to_core), (IS, to_half))):
-            all_of(i, buf, where)
+            part = LAYER if i < 2 else buf.shape[2]
+            all_of(i, buf.at[:, :, pl.ds(0, part), :], where)
 
         @pl.when(is_outer)
         def _():
             all_of(4, WS, to_half)
 
-    pl.semaphore_wait(barrier, 34)
-
-    for load in loads[:2]:
-        load.wait()
+    def no_padding(v, c):
+        for k in range(STEPS):
+            HL[k, v, LAYER:ROWS, :] = jnp.zeros((ROWS - LAYER, 128), F32)
+            HR[k, v, LAYER:ROWS, :] = jnp.zeros((ROWS - LAYER, 128), F32)
+        return c
+
+    lax.fori_loop(0, NV, no_padding, 0)
+    pl.semaphore_wait(barrier, 26)
+
+    loads[0].wait()
 
     def first_send(v, c):
+        load_vector(v).wait()
         for a in range(AZL):
             at = v * BLK + a * ROWS
             X[0, pl.ds(pl.multiple_of(at, 8), RC), :] = raw_c[pl.ds(v * (RC * AZL) + a, RC, stride=AZL), :]
@@ -157,7 +175,7 @@
         return c
 
     lax.fori_loop(0, NV, first_send, 0)
-    for load in loads[2:]:
+    for load in loads[1:]:
         load.wait()
 
     for a in range(AZL):
@@ -173,10 +191,7 @@
     STG[RC:ROWS, :] = shell_rows
     row64 = lax.broadcasted_iota(jnp.int32, (64, 128), 0)
     lane64 = lax.broadcasted_iota(jnp.int32, (64, 128), 1)
-    iface = jnp.where(is_outer, 0, RC - 1)
     matrix = STG[...]
-    matrix = jnp.where((lane64 == 56) & (row64 == iface), -1.0, matrix)
-    matrix = jnp.where((lane64 == 57) & (row64 == RC), -1.0, matrix)
     matrix = jnp.where((lane64 == 58) & (row64 == RC - 1), -outer, matrix)
     high = rounded(matrix)
     W[...] = jnp.concatenate([high + pltpu.roll(high, 64, axis=1), matrix - high], axis=1).astype(BF16)
@@ -191,37 +206,54 @@
     def apply(k):
         def body(v, moments):
             base = v * BLK
-            for copy in exchange(k, v):
-                copy.wait_recv()
-
-            @pl.when(grp == 0)
-            def _():
-                wall_copy(k, v).wait_recv()
-
+            from_left_slab, from_right_slab, from_core, from_half = exchange(k, v)
+            from_core.wait_recv()
             own = [X[k, pl.ds(pl.multiple_of(base + a * ROWS, 8), ROWS), :] for a in range(AZL)]
-            got, far = IR[k, v], WR[k, v]
+            wet_rows = [raw_w[a : a + 1, :] for a in range(AZL)]
             spread = []
             for a in range(AZL):
-                wet_row = raw_w[a : a + 1, :]
-                wall = jnp.where(is_outer, own[a][RC - 1 : RC], far[a : a + 1])
-                skin = own[a][RC : RC + 1]
-                extra = jnp.where(row == 0, got[a : a + 1], 0.0)
-                extra = jnp.where(row == 1, wet_row * wall, extra)
-                extra = jnp.where(row == 2, wet_row * skin, extra)
+                extra = jnp.where(row == 2, wet_rows[a] * own[a][RC : RC + 1], 0.0)
                 spread.append(jnp.concatenate([own[a], extra], axis=0))
             wide = jnp.concatenate(spread, axis=1)
             high = rounded(wide)
             stacked = jnp.concatenate([high, wide - high, high], axis=0).astype(BF16)
             mixed = jnp.dot(W[:, 0:192], stacked, preferred_element_type=F32)
+            part = []
             for a in range(AZL):
                 side = SB[k, v, a * ROWS : (a + 1) * ROWS, :]
-                before = HL[k, v] if a == 0 else own[a - 1]
-                after = HR[k, v] if a == AZL - 1 else own[a + 1]
                 lower = pltpu.roll(jnp.where(last_lane, side * from_left, own[a]), 1, axis=1)
                 upper = pltpu.roll(jnp.where(first_lane, side * from_right, own[a]), 127, axis=1)
-                new = mixed[0:ROWS, a * 128 : (a + 1) * 128] + DG[a] * own[a]
-                new = new - ((before + after) + (lower + upper))
-                X[k + 1, pl.ds(pl.multiple_of(base + a * ROWS, 8), ROWS), :] = new
+                value = mixed[0:ROWS, a * 128 : (a + 1) * 128] + DG[a] * own[a] - (lower + upper)
+                if a > 0:
+                    value = value - own[a - 1]
+                if a < AZL - 1:
+                    value = value - own[a + 1]
+                part.append(value)
+
+            from_left_slab.wait_recv()
+            from_right_slab.wait_recv()
+            from_half.wait_recv()
+
+            @pl.when(grp == 0)
+            def _():
+                wall_copy(k, v).wait_recv()
+
+            got, far = IR[k, v], WR[k, v]
+            for a in range(AZL):
+                value = part[a]
+                if a == 0:
+                    value = value - HL[k, v]
+                if a == AZL - 1:
+                    value = value - HR[k, v]
+                wall = jnp.where(is_outer, own[a][RC - 1 : RC], far[a : a + 1])
+                at = base + a * ROWS
+                top = value[0:8] - jnp.where(row == 0, outer * got[a : a + 1], 0.0)
+                edge = value[40:48] - jnp.where(row == 7, share * got[a : a + 1], 0.0)
+                skin = value[48:56] - jnp.where(row == 0, wet_rows[a] * wall, 0.0)
+                X[k + 1, pl.ds(pl.multiple_of(at, 8), 8), :] = top
+                X[k + 1, pl.ds(pl.multiple_of(at + 8, 8), 32), :] = value[8:40]
+                X[k + 1, pl.ds(pl.multiple_of(at + 40, 8), 8), :] = edge
+                X[k + 1, pl.ds(pl.multiple_of(at + 48, 8), 8), :] = skin
             if k + 1 < STEPS:
                 send(k + 1, v)
                 which = [(k, k, 16 * k), (k, k + 1, 16 * k + 8)]
@@ -254,42 +286,32 @@
             moments = jnp.where(lane == at + v, total, moments)
         return moments
 
-    def copy_of(i, d):
-        me, (s, where) = (me1, peer1(d)) if i % 2 == 0 else (me2, peer2(d))
-        out = pltpu.make_async_remote_copy(
-            RX.at[i, me], RX.at[i, me], sum_send.at[i, d], sum_recv.at[i, me], device_id=where, device_id_type=MESH
+    def sum_copy(i, stage, d):
+        at = place_in(stage)
+        return pltpu.make_async_remote_copy(
+            RX.at[i, stage, at], RX.at[i, stage, at], sum_send.at[i, stage], sum_recv.at[i, stage],
+            device_id=peer(stage, d)[1], device_id_type=MESH,
         )
-        back = pltpu.make_async_remote_copy(
-            RX.at[i, s], RX.at[i, s], sum_send.at[i, d], sum_recv.at[i, s], device_id=where, device_id_type=MESH
+
+    def sum_all(i, stage):
+        n = slots[stage] - 1
+        block = RX.at[i, stage, pl.ds(0, n)]
+        return pltpu.make_async_remote_copy(
+            block, block, sum_send.at[i, stage], sum_recv.at[i, stage],
+            device_id=peer(stage, 1)[1], device_id_type=MESH,
         )
-        return out, back
-
-    def sum_start(i, value):
-        RX[i, me1 if i % 2 == 0 else me2] = value
-
-        def start(d, c):
-            copy_of(i, d)[0].start()
-            return c
-
-        lax.fori_loop(1, 16, start, 0)
-
-    def sum_finish(i):
-        def wait(d, c):
-            copy_of(i, d)[1].wait_recv()
-            return c
-
-        lax.fori_loop(1, 16, wait, 0)
-        result = RX[i, 0]
-        for s in range(1, 16):
-            result += RX[i, s]
-        return result
-
-    def sum_drain(i):
-        def drain(d, c):
-            copy_of(i, d)[0].wait_send()
-            return c
-
-        lax.fori_loop(1, 16, drain, 0)
+
+    def sum_start(i, stage, value):
+        RX[i, stage, place_in(stage)] = value
+        for d in range(1, slots[stage]):
+            sum_copy(i, stage, d).start()
+
+    def sum_finish(i, stage):
+        sum_all(i, stage).wait_recv()
+        terms = [RX[i, stage, s] for s in range(slots[stage])]
+        while len(terms) > 1:
+            terms = [terms[q] + terms[q + 1] for q in range(0, len(terms), 2)]
+        return terms[0]
 
     def prepare(r, c):
         for half in range(2):
@@ -308,15 +330,16 @@
     early = lax.fori_loop(0, NV, apply(0), zero8)
     early = lax.fori_loop(0, NV, apply(1), early)
     early = lax.fori_loop(0, NV, lambda v, m: products([(2, 2, 32)], v, m), early)
-    sum_start(0, early)
+    sum_start(0, 2, early)
+    sum_start(0, 0, sum_finish(0, 2))
     late = lax.fori_loop(0, NV, apply(2), zero8)
-    sum_start(2, late)
-    early = sum_finish(0)
-    sum_start(1, early)
+    sum_start(1, 2, late)
+    sum_start(1, 0, sum_finish(1, 2))
+    sum_start(0, 1, sum_finish(0, 0))
     lax.fori_loop(0, 27, prepare, 0, unroll=3)
-    late = sum_finish(2)
-    sum_start(3, late)
-    gram = sum_finish(1)
+    sum_start(1, 1, sum_finish(1, 0))
+    gram = sum_finish(0, 1)
+
     shifted = pltpu.roll(gram, 120, axis=1) + THETA * gram
     table = []
     for i in range(STEPS):
@@ -327,7 +350,11 @@
         at, r = p // 8, p % 8
         if p == 16:
             lax.fori_loop(27, 54, prepare, 0, unroll=3)
-            table[2] = table[2] + sum_finish(3)
+            for k in range(STEPS):
+                sent(k)
+            for i, stage in ((0, 2), (0, 0), (0, 1), (1, 2), (1, 0)):
+                sum_all(i, stage).wait_send()
+            table[2] = table[2] + sum_finish(1, 1)
         pivot_row = table[at][r : r + 1, :]
         scaled = pivot_row * (1.0 / pivot_row[:, p : p + 1])
         for i in range(STEPS):
@@ -348,10 +375,7 @@
     mix = square.T[0:16, :]
     high = rounded(mix)
     MIX[...] = high + pltpu.roll(high, 32, axis=1) + pltpu.roll(mix - high, 64, axis=1)
-    for k in range(STEPS):
-        sent(k)
-    for i in range(4):
-        sum_drain(i)
+    sum_all(1, 1).wait_send()
 
 
 PIECES = 4
@@ -380,7 +404,7 @@
         return copies
 
     each = RC // PIECES
-    lax.fori_loop(0, RS, rows_of(RC, RS, o_ss, o_rs), 0, unroll=2)
+    lax.fori_loop(0, RS, rows_of(RC, RS, o_ss, o_rs), 0, unroll=True)
     small = [
         pltpu.make_async_copy(o_ss, sol_s, sem.at[2]),
         pltpu.make_async_copy(o_rs, res_s, sem.at[3]),
@@ -388,7 +412,7 @@
     for copy in small:
         copy.start()
     for i in range(PIECES):
-        lax.fori_loop(i * each, (i + 1) * each, rows_of(0, RC, o_sc, o_rc), 0, unroll=4)
+        lax.fori_loop(i * each, (i + 1) * each, rows_of(0, RC, o_sc, o_rc), 0, unroll=True)
         for copy in piece(i, o_sc, sol_c, 0, each * AZL) + piece(i, o_rc, res_c, 1, each * AZL):
             copy.start()
     for copy in small:
@@ -429,7 +453,7 @@
             pltpu.VMEM((64, 256), BF16),
             pltpu.VMEM((64, 128), F32),
             pltpu.VMEM((128, 128), F32),
-            pltpu.VMEM((4, 16, 8, 128), F32),
+            pltpu.VMEM((2, 3, 16, 8, 128), F32),
             pltpu.VMEM((nc, 128), F32),
             pltpu.VMEM((ns, 128), F32),
             pltpu.VMEM((RC * AZL, 128), F32),
@@ -437,11 +461,12 @@
             pltpu.VMEM((AZL, 128), F32),
             pltpu.VMEM((RC, RC), F32),
             pltpu.VMEM((RS, RS), F32),
-            pltpu.SemaphoreType.DMA((7,)),
+            pltpu.SemaphoreType.DMA((6,)),
+            pltpu.SemaphoreType.DMA((NV,)),
             pltpu.SemaphoreType.DMA((STEPS, 5)),
             pltpu.SemaphoreType.DMA((STEPS, NV, 5)),
-            pltpu.SemaphoreType.DMA((4, 16)),
-            pltpu.SemaphoreType.DMA((4, 16)),
+            pltpu.SemaphoreType.DMA((2, 3)),
+            pltpu.SemaphoreType.DMA((2, 3)),
         ],
         compiler_params=pltpu.CompilerParams(
             collective_id=0, has_side_effects=True, vmem_limit_bytes=22 * 1024 * 1024

time: 54.8 us -> 52.7 us (0.962)
  Pallas kernels: 54.1 us -> 52 us
    pallas_call x1, Pallas kernels: 3.63 us -> 2.01 us  [per_device(): pl.pallas_call(finish_kernel, out_shape=(jax.ShapeDtypeStruct((nc, 128),...]
where the time goes in v3:
time: 52.7 us; the launch traced here: 52.6 us
  Pallas kernels  52 us (99%)
  between operations  0.64 us (1%)
    pallas_call x1, Pallas kernels, per_device(): pl.pallas_call(kernel, out_shape=(pltpu.VMEM((2 * (RC + RS), 96, 256), BF...  50 us
    pallas_call x1, Pallas kernels, per_device(): pl.pallas_call(finish_kernel, out_shape=(jax.ShapeDtypeStruct((nc, 128),...  2.01 us

profile of v3, /device:TPU:1, one launch (start us, length us, event | category | flops | bytes accessed | tf_op | source)
XLA Modules:
  0.0 52.6 jit_solution(8261080443103219851)
XLA Ops:
  0.6 50.0 %block_cg.1 = (bf16[108,96,256]{2,1,0:T(8,128)(2,1)S(1)}, f32[16,128]{1,0:T(8,128)S(1)}) custom-call(f32[1536,128]{1,0:T(8,128)} %bitcast.9, f32[192,128]{1,0:T(8,128)} %bitcast.10, f32[48,48]{1,0:T(8,128)} %bitcast.12, f32[6,6]{1,0:T(8,128)} %shm.1, f32[192,128]{1,0:T(8,128)} %bitcast.11, f32[24,128]{1,0:T(8,128)} %bitcast.13, f32[4,128]{1,0:T(4,128)} %wet.1), custom_call_target="tpu_custom_call" | custom-call | tf_op jit(solution)/shard_map/block_cg/pallas_call | solution.py:438
  50.6 2.0 %combine_basis.1 = (f32[1536,128]{1,0:T(8,128)}, f32[1536,128]{1,0:T(8,128)}, f32[192,128]{1,0:T(8,128)}, f32[192,128]{1,0:T(8,128)}) custom-call(bf16[108,96,256]{2,1,0:T(8,128)(2,1)S(1)} %get-tuple-element.10.T, f32[16,128]{1,0:T(8,128)S(1)} %get-tuple-element.11.MIX), custom_call_target="tpu_custom_call" | custom-call | tf_op jit(solution)/shard_map/combine_basis/pallas_call | solution.py:476

commit v4 on v3

--- a/solution.py
+++ b/solution.py
@@ -28,7 +28,7 @@
     T, MIX,
     X, HL, HR, SB, IS, IR, WS, WR, DG, W, STG, ACC, RX,
     raw_c, raw_s, raw_d, raw_sd, raw_w, raw_cm, raw_sm,
-    in_sem, vec_sem, send_sem, recv_sem, sum_send, sum_recv,
+    in_sem, vec_sem, send_sem, recv_sem, sum_send, sum_recv, word,
 ):
     grp = lax.axis_index("grp")
     az = lax.axis_index("az")
@@ -77,16 +77,24 @@
             return g * 4 + z, {"grp": g, "az": px * 16 + z * 4 + py, "ax": ax}
         return 1 - ax, {"grp": grp, "az": az, "ax": 1 - ax}
 
+    def far(step, side):
+        apart = 2 ** (step + 1)
+        return {"grp": grp, "az": lax.rem(az + (apart if side == 0 else naz - apart), naz), "ax": ax}
+
+    def pass_word(step):
+        for side in range(2):
+            pl.semaphore_signal(word.at[step, side], inc=1, device_id=far(step, side), device_id_type=MESH)
+
+    def hear_word(step):
+        for side in range(2):
+            pl.semaphore_wait(word.at[step, side], 1)
+
     to_right = {"grp": grp, "az": right, "ax": ax}
     to_left = {"grp": grp, "az": left, "ax": ax}
     to_core = {"grp": grp, "az": az, "ax": 1 - ax}
     to_half = {"grp": 1 - grp, "az": az, "ax": ax}
     for where in (to_right, to_left, to_core, to_half):
         hello(where)
-
-    for stage in range(2):
-        for d in range(1, slots[stage]):
-            hello(peer(stage, d)[1])
 
     outer = (grp == 1).astype(F32)
     is_outer = grp == 1
@@ -158,7 +166,7 @@
         return c
 
     lax.fori_loop(0, NV, no_padding, 0)
-    pl.semaphore_wait(barrier, 26)
+    pl.semaphore_wait(barrier, 4)
 
     loads[0].wait()
 
@@ -256,10 +264,15 @@
                 X[k + 1, pl.ds(pl.multiple_of(at + 48, 8), 8), :] = skin
             if k + 1 < STEPS:
                 send(k + 1, v)
-                which = [(k, k, 16 * k), (k, k + 1, 16 * k + 8)]
-            else:
-                which = [(k, k + 1, 16)]
-            return products(which, v, moments)
+            for hear, tell, when in (((None, 0, 0),), ((0, 1, 0), (1, 2, NV - 1)), ((2, 3, 4),))[k]:
+
+                @pl.when(v == when)
+                def _(hear=hear, tell=tell):
+                    if hear is not None:
+                        hear_word(hear)
+                    pass_word(tell)
+
+            return products([(k, k, 16 * k), (k, k + 1, 16 * k + 8)], v, moments)
 
         return body
 
@@ -286,29 +299,29 @@
             moments = jnp.where(lane == at + v, total, moments)
         return moments
 
-    def sum_copy(i, stage, d):
+    def sum_copy(stage, d):
         at = place_in(stage)
         return pltpu.make_async_remote_copy(
-            RX.at[i, stage, at], RX.at[i, stage, at], sum_send.at[i, stage], sum_recv.at[i, stage],
+            RX.at[stage, at], RX.at[stage, at], sum_send.at[stage], sum_recv.at[stage],
             device_id=peer(stage, d)[1], device_id_type=MESH,
         )
 
-    def sum_all(i, stage):
+    def sum_all(stage):
         n = slots[stage] - 1
-        block = RX.at[i, stage, pl.ds(0, n)]
+        block = RX.at[stage, pl.ds(0, n)]
         return pltpu.make_async_remote_copy(
-            block, block, sum_send.at[i, stage], sum_recv.at[i, stage],
+            block, block, sum_send.at[stage], sum_recv.at[stage],
             device_id=peer(stage, 1)[1], device_id_type=MESH,
         )
 
-    def sum_start(i, stage, value):
-        RX[i, stage, place_in(stage)] = value
+    def sum_start(stage, value):
+        RX[stage, place_in(stage)] = value
         for d in range(1, slots[stage]):
-            sum_copy(i, stage, d).start()
-
-    def sum_finish(i, stage):
-        sum_all(i, stage).wait_recv()
-        terms = [RX[i, stage, s] for s in range(slots[stage])]
+            sum_copy(stage, d).start()
+
+    def sum_finish(stage):
+        sum_all(stage).wait_recv()
+        terms = [RX[stage, s] for s in range(slots[stage])]
         while len(terms) > 1:
             terms = [terms[q] + terms[q + 1] for q in range(0, len(terms), 2)]
         return terms[0]
@@ -327,18 +340,22 @@
         return c
 
     zero8 = jnp.zeros((8, 128), F32)
-    early = lax.fori_loop(0, NV, apply(0), zero8)
-    early = lax.fori_loop(0, NV, apply(1), early)
-    early = lax.fori_loop(0, NV, lambda v, m: products([(2, 2, 32)], v, m), early)
-    sum_start(0, 2, early)
-    sum_start(0, 0, sum_finish(0, 2))
-    late = lax.fori_loop(0, NV, apply(2), zero8)
-    sum_start(1, 2, late)
-    sum_start(1, 0, sum_finish(1, 2))
-    sum_start(0, 1, sum_finish(0, 0))
+    moments = zero8
+    for k in range(STEPS):
+        moments = lax.fori_loop(0, NV, apply(k), moments)
+    sum_start(2, moments)
+    hear_word(3)
+    pl.semaphore_signal(word.at[4, 0], inc=1, device_id=to_half, device_id_type=MESH)
+    sum_start(0, sum_finish(2))
     lax.fori_loop(0, 27, prepare, 0, unroll=3)
-    sum_start(1, 1, sum_finish(1, 0))
-    gram = sum_finish(0, 1)
+    for k in range(STEPS):
+        sent(k)
+    pl.semaphore_wait(word.at[4, 0], 1)
+    sum_start(1, sum_finish(0))
+    lax.fori_loop(27, 54, prepare, 0, unroll=3)
+    for stage in (2, 0):
+        sum_all(stage).wait_send()
+    gram = sum_finish(1)
 
     shifted = pltpu.roll(gram, 120, axis=1) + THETA * gram
     table = []
@@ -346,21 +363,27 @@
         left_part = shifted if i == 0 else pltpu.roll(shifted, 128 - 8 * i, axis=1)
         right_part = pltpu.roll(gram, 24 - 8 * i, axis=1)
         table.append(jnp.where(lane < 24, left_part, jnp.where(lane < 32, right_part, 0.0)))
-    for p in range(8 * STEPS):
+    full = (8, 128)
+
+    def over(part):
+        return jnp.broadcast_to(part, full)
+
+    for p in range(0, 8 * STEPS, 2):
         at, r = p // 8, p % 8
-        if p == 16:
-            lax.fori_loop(27, 54, prepare, 0, unroll=3)
-            for k in range(STEPS):
-                sent(k)
-            for i, stage in ((0, 2), (0, 0), (0, 1), (1, 2), (1, 0)):
-                sum_all(i, stage).wait_send()
-            table[2] = table[2] + sum_finish(1, 1)
-        pivot_row = table[at][r : r + 1, :]
-        scaled = pivot_row * (1.0 / pivot_row[:, p : p + 1])
+        first = [over(t[:, p : p + 1]) for t in table]
+        second = [over(t[:, p + 1 : p + 2]) for t in table]
+        inverse = 1.0 / over(first[at][r : r + 1, :])
+        row_a = over(table[at][r : r + 1, :]) * inverse
+        ratio = over(second[at][r : r + 1, :]) * inverse
+        below = over(first[at][r + 1 : r + 2, :])
+        row_b = over(table[at][r + 1 : r + 2, :]) - below * row_a
+        row_b = row_b * (1.0 / (over(second[at][r + 1 : r + 2, :]) - below * ratio))
+        row_a = row_a - ratio * row_b
         for i in range(STEPS):
-            column = table[i][:, p : p + 1]
-            reduced = table[i] - column * scaled
-            table[i] = jnp.where(row == r, scaled, reduced) if i == at else reduced
+            reduced = table[i] - first[i] * row_a - second[i] * row_b
+            if i == at:
+                reduced = jnp.where(row == r, row_a, jnp.where(row == r + 1, row_b, reduced))
+            table[i] = reduced
 
     y = [jnp.where(lane < 8, pltpu.roll(t, 104, axis=1), 0.0) for t in table]
     eye = jnp.where(lane == row, 1.0, 0.0)
@@ -375,7 +398,7 @@
     mix = square.T[0:16, :]
     high = rounded(mix)
     MIX[...] = high + pltpu.roll(high, 32, axis=1) + pltpu.roll(mix - high, 64, axis=1)
-    sum_all(1, 1).wait_send()
+    sum_all(1).wait_send()
 
 
 PIECES = 4
@@ -453,7 +476,7 @@
             pltpu.VMEM((64, 256), BF16),
             pltpu.VMEM((64, 128), F32),
             pltpu.VMEM((128, 128), F32),
-            pltpu.VMEM((2, 3, 16, 8, 128), F32),
+            pltpu.VMEM((3, 16, 8, 128), F32),
             pltpu.VMEM((nc, 128), F32),
             pltpu.VMEM((ns, 128), F32),
             pltpu.VMEM((RC * AZL, 128), F32),
@@ -465,8 +488,9 @@
             pltpu.SemaphoreType.DMA((NV,)),
             pltpu.SemaphoreType.DMA((STEPS, 5)),
             pltpu.SemaphoreType.DMA((STEPS, NV, 5)),
-            pltpu.SemaphoreType.DMA((2, 3)),
-            pltpu.SemaphoreType.DMA((2, 3)),
+            pltpu.SemaphoreType.DMA((3,)),
+            pltpu.SemaphoreType.DMA((3,)),
+            pltpu.SemaphoreType.REGULAR((5, 2)),
         ],
         compiler_params=pltpu.CompilerParams(
             collective_id=0, has_side_effects=True, vmem_limit_bytes=22 * 1024 * 1024

time: 52.7 us -> 50.5 us (0.958)
  Pallas kernels: 52 us -> 49.7 us
    pallas_call x1, Pallas kernels: 50 us -> 47.7 us  [per_device(): pl.pallas_call(kernel, out_shape=(pltpu.VMEM((2 * (RC + RS), 96, 256), BF...]
where the time goes in v4:
time: 50.5 us; the launch traced here: 50.4 us
  Pallas kernels  49.7 us (98%)
  between operations  0.64 us (1%)
    pallas_call x1, Pallas kernels, per_device(): pl.pallas_call(kernel, out_shape=(pltpu.VMEM((2 * (RC + RS), 96, 256), BF...  47.7 us
    pallas_call x1, Pallas kernels, per_device(): pl.pallas_call(finish_kernel, out_shape=(jax.ShapeDtypeStruct((nc, 128),...  2.01 us

profile of v4, /device:TPU:1, one launch (start us, length us, event | category | flops | bytes accessed | tf_op | source)
XLA Modules:
  0.0 50.4 jit_solution(3792553799429914083)
XLA Ops:
  0.6 47.7 %block_cg.1 = (bf16[108,96,256]{2,1,0:T(8,128)(2,1)S(1)}, f32[16,128]{1,0:T(8,128)S(1)}) custom-call(f32[1536,128]{1,0:T(8,128)} %bitcast.9, f32[192,128]{1,0:T(8,128)} %bitcast.10, f32[48,48]{1,0:T(8,128)} %bitcast.12, f32[6,6]{1,0:T(8,128)} %shm.1, f32[192,128]{1,0:T(8,128)} %bitcast.11, f32[24,128]{1,0:T(8,128)} %bitcast.13, f32[4,128]{1,0:T(4,128)} %wet.1), custom_call_target="tpu_custom_call" | custom-call | tf_op jit(solution)/shard_map/block_cg/pallas_call | solution.py:461
  48.4 2.0 %combine_basis.1 = (f32[1536,128]{1,0:T(8,128)}, f32[1536,128]{1,0:T(8,128)}, f32[192,128]{1,0:T(8,128)}, f32[192,128]{1,0:T(8,128)}) custom-call(bf16[108,96,256]{2,1,0:T(8,128)(2,1)S(1)} %get-tuple-element.10.T, f32[16,128]{1,0:T(8,128)S(1)} %get-tuple-element.11.MIX), custom_call_target="tpu_custom_call" | custom-call | tf_op jit(solution)/shard_map/combine_basis/pallas_call | solution.py:500

commit v5 on v4

--- a/solution.py
+++ b/solution.py
@@ -40,6 +40,46 @@
     pz = lax.rem(az // 4, 4)
     py = lax.rem(az, 4)
 
+    barrier = pltpu.get_barrier_semaphore()
+
+    def hello(where):
+        pl.semaphore_signal(barrier, inc=1, device_id=where, device_id_type=MESH)
+
+    here1 = px * 4 + py
+    here2 = grp * 4 + pz
+    slots = (16, 8, 2)
+
+    def place_in(stage):
+        return (here1, here2, ax)[stage]
+
+    def peer(stage, d):
+        if stage == 0:
+            x, y = lax.rem(px + d // 4, 4), lax.rem(py + d % 4, 4)
+            return x * 4 + y, {"grp": grp, "az": x * 16 + pz * 4 + y, "ax": ax}
+        if stage == 1:
+            g, z = lax.rem(grp + d // 4, 2), lax.rem(pz + d % 4, 4)
+            return g * 4 + z, {"grp": g, "az": px * 16 + z * 4 + py, "ax": ax}
+        return 1 - ax, {"grp": grp, "az": az, "ax": 1 - ax}
+
+    def far(step, side):
+        apart = 2 ** (step + 1)
+        return {"grp": grp, "az": lax.rem(az + (apart if side == 0 else naz - apart), naz), "ax": ax}
+
+    def pass_word(step):
+        for side in range(2):
+            pl.semaphore_signal(word.at[step, side], inc=1, device_id=far(step, side), device_id_type=MESH)
+
+    def hear_word(step):
+        for side in range(2):
+            pl.semaphore_wait(word.at[step, side], 1)
+
+    to_right = {"grp": grp, "az": right, "ax": ax}
+    to_left = {"grp": grp, "az": left, "ax": ax}
+    to_core = {"grp": grp, "az": az, "ax": 1 - ax}
+    to_half = {"grp": 1 - grp, "az": az, "ax": ax}
+    for where in (to_right, to_left, to_core, to_half):
+        hello(where)
+
     loads = [
         pltpu.make_async_copy(src, dst, in_sem.at[i])
         for i, (src, dst) in enumerate(
@@ -55,46 +95,6 @@
         load_vector(v).start()
     for load in loads[1:]:
         load.start()
-
-    barrier = pltpu.get_barrier_semaphore()
-
-    def hello(where):
-        pl.semaphore_signal(barrier, inc=1, device_id=where, device_id_type=MESH)
-
-    here1 = px * 4 + py
-    here2 = grp * 4 + pz
-    slots = (16, 8, 2)
-
-    def place_in(stage):
-        return (here1, here2, ax)[stage]
-
-    def peer(stage, d):
-        if stage == 0:
-            x, y = lax.rem(px + d // 4, 4), lax.rem(py + d % 4, 4)
-            return x * 4 + y, {"grp": grp, "az": x * 16 + pz * 4 + y, "ax": ax}
-        if stage == 1:
-            g, z = lax.rem(grp + d // 4, 2), lax.rem(pz + d % 4, 4)
-            return g * 4 + z, {"grp": g, "az": px * 16 + z * 4 + py, "ax": ax}
-        return 1 - ax, {"grp": grp, "az": az, "ax": 1 - ax}
-
-    def far(step, side):
-        apart = 2 ** (step + 1)
-        return {"grp": grp, "az": lax.rem(az + (apart if side == 0 else naz - apart), naz), "ax": ax}
-
-    def pass_word(step):
-        for side in range(2):
-            pl.semaphore_signal(word.at[step, side], inc=1, device_id=far(step, side), device_id_type=MESH)
-
-    def hear_word(step):
-        for side in range(2):
-            pl.semaphore_wait(word.at[step, side], 1)
-
-    to_right = {"grp": grp, "az": right, "ax": ax}
-    to_left = {"grp": grp, "az": left, "ax": ax}
-    to_core = {"grp": grp, "az": az, "ax": 1 - ax}
-    to_half = {"grp": 1 - grp, "az": az, "ax": ax}
-    for where in (to_right, to_left, to_core, to_half):
-        hello(where)
 
     outer = (grp == 1).astype(F32)
     is_outer = grp == 1
@@ -136,9 +136,12 @@
             WS.at[k, v], WR.at[k, v], send_sem.at[k, 4], recv_sem.at[k, v, 4], device_id=to_half, device_id_type=MESH
         )
 
-    def send(k, v):
-        rows_to_send(k, v)
-        for copy in exchange(k, v):
+    def send_layers(k, v):
+        for copy in exchange(k, v)[:2]:
+            copy.start()
+
+    def send_rest(k, v):
+        for copy in exchange(k, v)[2:]:
             copy.start()
 
         @pl.when(is_outer)
@@ -159,18 +162,9 @@
         def _():
             all_of(4, WS, to_half)
 
-    def no_padding(v, c):
-        for k in range(STEPS):
-            HL[k, v, LAYER:ROWS, :] = jnp.zeros((ROWS - LAYER, 128), F32)
-            HR[k, v, LAYER:ROWS, :] = jnp.zeros((ROWS - LAYER, 128), F32)
-        return c
-
-    lax.fori_loop(0, NV, no_padding, 0)
-    pl.semaphore_wait(barrier, 4)
-
     loads[0].wait()
 
-    def first_send(v, c):
+    def settle(v, c):
         load_vector(v).wait()
         for a in range(AZL):
             at = v * BLK + a * ROWS
@@ -179,9 +173,20 @@
                 [raw_s[pl.ds(v * (RS * AZL) + a, RS, stride=AZL), :], jnp.zeros((2, 128), F32)], axis=0
             )
             X[0, pl.ds(pl.multiple_of(at + RC, 8), 8), :] = tail
-        send(0, v)
+        rows_to_send(0, v)
+        for k in range(STEPS):
+            HL[k, v, LAYER:ROWS, :] = jnp.zeros((ROWS - LAYER, 128), F32)
+            HR[k, v, LAYER:ROWS, :] = jnp.zeros((ROWS - LAYER, 128), F32)
         return c
 
+    lax.fori_loop(0, NV, settle, 0)
+
+    def first_send(v, c):
+        send_layers(0, v)
+        send_rest(0, v)
+        return c
+
+    pl.semaphore_wait(barrier, 4)
     lax.fori_loop(0, NV, first_send, 0)
     for load in loads[1:]:
         load.wait()
@@ -247,7 +252,7 @@
                 wall_copy(k, v).wait_recv()
 
             got, far = IR[k, v], WR[k, v]
-            for a in range(AZL):
+            for a in (0, AZL - 1, *range(1, AZL - 1)):
                 value = part[a]
                 if a == 0:
                     value = value - HL[k, v]
@@ -262,8 +267,13 @@
                 X[k + 1, pl.ds(pl.multiple_of(at + 8, 8), 32), :] = value[8:40]
                 X[k + 1, pl.ds(pl.multiple_of(at + 40, 8), 8), :] = edge
                 X[k + 1, pl.ds(pl.multiple_of(at + 48, 8), 8), :] = skin
+                if k + 1 < STEPS:
+                    IS[k + 1, v, a : a + 1, :] = jnp.where(is_outer, top[0:1], edge[7:8])
+                    WS[k + 1, v, a : a + 1, :] = edge[7:8]
+                    if a == AZL - 1:
+                        send_layers(k + 1, v)
             if k + 1 < STEPS:
-                send(k + 1, v)
+                send_rest(k + 1, v)
             for hear, tell, when in (((None, 0, 0),), ((0, 1, 0), (1, 2, NV - 1)), ((2, 3, 4),))[k]:
 
                 @pl.when(v == when)
@@ -368,22 +378,18 @@
     def over(part):
         return jnp.broadcast_to(part, full)
 
-    for p in range(0, 8 * STEPS, 2):
-        at, r = p // 8, p % 8
-        first = [over(t[:, p : p + 1]) for t in table]
-        second = [over(t[:, p + 1 : p + 2]) for t in table]
-        inverse = 1.0 / over(first[at][r : r + 1, :])
-        row_a = over(table[at][r : r + 1, :]) * inverse
-        ratio = over(second[at][r : r + 1, :]) * inverse
-        below = over(first[at][r + 1 : r + 2, :])
-        row_b = over(table[at][r + 1 : r + 2, :]) - below * row_a
-        row_b = row_b * (1.0 / (over(second[at][r + 1 : r + 2, :]) - below * ratio))
-        row_a = row_a - ratio * row_b
-        for i in range(STEPS):
-            reduced = table[i] - first[i] * row_a - second[i] * row_b
-            if i == at:
-                reduced = jnp.where(row == r, row_a, jnp.where(row == r + 1, row_b, reduced))
-            table[i] = reduced
+    for at in range(STEPS):
+        columns = [[over(t[:, 8 * at + q : 8 * at + q + 1]) for t in table] for q in range(8)]
+        for r in range(8):
+            inverse = 1.0 / over(columns[r][at][r : r + 1, :])
+            scaled = over(table[at][r : r + 1, :]) * inverse
+            ratios = {q: over(columns[q][at][r : r + 1, :]) * inverse for q in range(r + 1, 8)}
+            for i in range(STEPS):
+                for q, ratio in ratios.items():
+                    reduced = columns[q][i] - columns[r][i] * ratio
+                    columns[q][i] = jnp.where(row == r, ratio, reduced) if i == at else reduced
+                reduced = table[i] - columns[r][i] * scaled
+                table[i] = jnp.where(row == r, scaled, reduced) if i == at else reduced
 
     y = [jnp.where(lane < 8, pltpu.roll(t, 104, axis=1), 0.0) for t in table]
     eye = jnp.where(lane == row, 1.0, 0.0)

time: 50.5 us -> 49.1 us (0.972)
  Pallas kernels: 49.7 us -> 48.3 us
    pallas_call x1, Pallas kernels: 47.7 us -> 46.3 us  [per_device(): pl.pallas_call(kernel, out_shape=(pltpu.VMEM((2 * (RC + RS), 96, 256), BF...]
where the time goes in v5:
time: 49.1 us; the launch traced here: 48.9 us
  Pallas kernels  48.3 us (98%)
  between operations  0.64 us (1%)
    pallas_call x1, Pallas kernels, per_device(): pl.pallas_call(kernel, out_shape=(pltpu.VMEM((2 * (RC + RS), 96, 256), BF...  46.3 us
    pallas_call x1, Pallas kernels, per_device(): pl.pallas_call(finish_kernel, out_shape=(jax.ShapeDtypeStruct((nc, 128),...  2.01 us

profile of v5, /device:TPU:1, one launch (start us, length us, event | category | flops | bytes accessed | tf_op | source)
XLA Modules:
  0.0 48.9 jit_solution(4012393867800211706)
XLA Ops:
  0.6 46.3 %block_cg.1 = (bf16[108,96,256]{2,1,0:T(8,128)(2,1)S(1)}, f32[16,128]{1,0:T(8,128)S(1)}) custom-call(f32[1536,128]{1,0:T(8,128)} %bitcast.9, f32[192,128]{1,0:T(8,128)} %bitcast.10, f32[48,48]{1,0:T(8,128)} %bitcast.12, f32[6,6]{1,0:T(8,128)} %shm.1, f32[192,128]{1,0:T(8,128)} %bitcast.11, f32[24,128]{1,0:T(8,128)} %bitcast.13, f32[4,128]{1,0:T(4,128)} %wet.1), custom_call_target="tpu_custom_call" | custom-call | tf_op jit(solution)/shard_map/block_cg/pallas_call | solution.py:467
  46.9 2.0 %combine_basis.1 = (f32[1536,128]{1,0:T(8,128)}, f32[1536,128]{1,0:T(8,128)}, f32[192,128]{1,0:T(8,128)}, f32[192,128]{1,0:T(8,128)}) custom-call(bf16[108,96,256]{2,1,0:T(8,128)(2,1)S(1)} %get-tuple-element.10.T, f32[16,128]{1,0:T(8,128)S(1)} %get-tuple-element.11.MIX), custom_call_target="tpu_custom_call" | custom-call | tf_op jit(solution)/shard_map/combine_basis/pallas_call | solution.py:506

commit v6 on v5

--- a/solution.py
+++ b/solution.py
@@ -324,9 +324,13 @@
             device_id=peer(stage, 1)[1], device_id_type=MESH,
         )
 
+    def hops(stage, d):
+        major, minor = d // 4, d % 4
+        return min(minor, 4 - minor) + (min(major, 4 - major) if stage == 0 else 4 * major)
+
     def sum_start(stage, value):
         RX[stage, place_in(stage)] = value
-        for d in range(1, slots[stage]):
+        for d in sorted(range(1, slots[stage]), key=lambda d: hops(stage, d), reverse=True):
             sum_copy(stage, d).start()
 
     def sum_finish(stage):
@@ -400,8 +404,9 @@
         -y[2],
     ]
     parts = [(y[k] if k < STEPS else zero8) + pltpu.roll(into[k], 8, axis=1) for k in range(4)]
-    square = jnp.concatenate(parts + [jnp.zeros((96, 128), F32)], axis=0)
-    mix = square.T[0:16, :]
+    square = jnp.concatenate(parts, axis=0)
+    turned = square.T[0:16, :]
+    mix = jnp.concatenate([turned, jnp.zeros((16, 96), F32)], axis=1)
     high = rounded(mix)
     MIX[...] = high + pltpu.roll(high, 32, axis=1) + pltpu.roll(mix - high, 64, axis=1)
     sum_all(1).wait_send()

time: 49.1 us -> 49 us (level)
  no operation moved by 1% of the time
where the time goes in v6:
time: 49 us; the launch traced here: 48.9 us
  Pallas kernels  48.3 us (99%)
  between operations  0.64 us (1%)
    pallas_call x1, Pallas kernels, per_device(): pl.pallas_call(kernel, out_shape=(pltpu.VMEM((2 * (RC + RS), 96, 256), BF...  46.3 us
    pallas_call x1, Pallas kernels, per_device(): pl.pallas_call(finish_kernel, out_shape=(jax.ShapeDtypeStruct((nc, 128),...  2.01 us

profile of v6, /device:TPU:1, one launch (start us, length us, event | category | flops | bytes accessed | tf_op | source)
XLA Modules:
  0.0 48.9 jit_solution(7890132895373301278)
XLA Ops:
  0.6 46.3 %block_cg.1 = (bf16[108,96,256]{2,1,0:T(8,128)(2,1)S(1)}, f32[16,128]{1,0:T(8,128)S(1)}) custom-call(f32[1536,128]{1,0:T(8,128)} %bitcast.9, f32[192,128]{1,0:T(8,128)} %bitcast.10, f32[48,48]{1,0:T(8,128)} %bitcast.12, f32[6,6]{1,0:T(8,128)} %shm.1, f32[192,128]{1,0:T(8,128)} %bitcast.11, f32[24,128]{1,0:T(8,128)} %bitcast.13, f32[4,128]{1,0:T(4,128)} %wet.1), custom_call_target="tpu_custom_call" | custom-call | tf_op jit(solution)/shard_map/block_cg/pallas_call | solution.py:472
  46.9 2.0 %combine_basis.1 = (f32[1536,128]{1,0:T(8,128)}, f32[1536,128]{1,0:T(8,128)}, f32[192,128]{1,0:T(8,128)}, f32[192,128]{1,0:T(8,128)}) custom-call(bf16[108,96,256]{2,1,0:T(8,128)(2,1)S(1)} %get-tuple-element.10.T, f32[16,128]{1,0:T(8,128)S(1)} %get-tuple-element.11.MIX), custom_call_target="tpu_custom_call" | custom-call | tf_op jit(solution)/shard_map/combine_basis/pallas_call | solution.py:511

commit v7 on v6

--- a/solution.py
+++ b/solution.py
@@ -274,7 +274,7 @@
                         send_layers(k + 1, v)
             if k + 1 < STEPS:
                 send_rest(k + 1, v)
-            for hear, tell, when in (((None, 0, 0),), ((0, 1, 0), (1, 2, NV - 1)), ((2, 3, 4),))[k]:
+            for hear, tell, when in (((None, 0, 0),), ((0, 1, 0), (1, 2, 5)), ((2, 3, 2),))[k]:
 
                 @pl.when(v == when)
                 def _(hear=hear, tell=tell):

time: 49 us -> 49 us (level)
  no operation moved by 1% of the time
where the time goes in v7:
time: 49 us; the launch traced here: 48.9 us
  Pallas kernels  48.3 us (99%)
  between operations  0.64 us (1%)
    pallas_call x1, Pallas kernels, per_device(): pl.pallas_call(kernel, out_shape=(pltpu.VMEM((2 * (RC + RS), 96, 256), BF...  46.3 us
    pallas_call x1, Pallas kernels, per_device(): pl.pallas_call(finish_kernel, out_shape=(jax.ShapeDtypeStruct((nc, 128),...  2.01 us

profile of v7, /device:TPU:1, one launch (start us, length us, event | category | flops | bytes accessed | tf_op | source)
XLA Modules:
  0.0 48.9 jit_solution(17469405748506422291)
XLA Ops:
  0.6 46.3 %block_cg.1 = (bf16[108,96,256]{2,1,0:T(8,128)(2,1)S(1)}, f32[16,128]{1,0:T(8,128)S(1)}) custom-call(f32[1536,128]{1,0:T(8,128)} %bitcast.9, f32[192,128]{1,0:T(8,128)} %bitcast.10, f32[48,48]{1,0:T(8,128)} %bitcast.12, f32[6,6]{1,0:T(8,128)} %shm.1, f32[192,128]{1,0:T(8,128)} %bitcast.11, f32[24,128]{1,0:T(8,128)} %bitcast.13, f32[4,128]{1,0:T(4,128)} %wet.1), custom_call_target="tpu_custom_call" | custom-call | tf_op jit(solution)/shard_map/block_cg/pallas_call | solution.py:472
  46.9 2.0 %combine_basis.1 = (f32[1536,128]{1,0:T(8,128)}, f32[1536,128]{1,0:T(8,128)}, f32[192,128]{1,0:T(8,128)}, f32[192,128]{1,0:T(8,128)}) custom-call(bf16[108,96,256]{2,1,0:T(8,128)(2,1)S(1)} %get-tuple-element.10.T, f32[16,128]{1,0:T(8,128)S(1)} %get-tuple-element.11.MIX), custom_call_target="tpu_custom_call" | custom-call | tf_op jit(solution)/shard_map/combine_basis/pallas_call | solution.py:511
